TPU v7x, 128 devices: a whole 4x4x4 slice. The times are simulated.
128 devices in a mesh: dp: 2 (over x_lo), mp: 64 (over z, y, x_hi, core).
Axes of the slice: x: 4 (x_hi: 2, x_lo: 2; x = x_hi * 2 + x_lo), y: 4, z: 4, core: 2. Of those that a mesh axis runs over, the one named last changes fastest.
Arguments:
- grad_partials: bfloat16 [2, 64, 1024, 1024], P('dp', None, 'mp'), may hold values from -60 to 60
- second_moment: float32 [64, 1024, 1024], P('mp', None, 'dp'), may hold values from 0.1 to 10
- left_root: float32 [64, 1024, 1024], P('mp', 'dp'), may hold values from -1 to 3
- right_root: float32 [64, 1024, 1024], P('mp', None, 'dp'), may hold values from -1 to 3
- left_stat: float32 [64, 1024, 1024], P('mp', 'dp'), may hold values from -6 to 6
- right_stat: float32 [64, 1024, 1024], P('mp', None, 'dp'), may hold values from -6 to 6
Outputs:
- update: float32 [64, 1024, 1024], P(None, 'mp', 'dp')
- moment_new: float32 [64, 1024, 1024], P('mp', None, 'dp')
- left_new: float32 [64, 1024, 1024], P('mp', 'dp')
- right_new: float32 [64, 1024, 1024], P('mp', None, 'dp')
All inputs are finite; a program needn't handle non-finite values.
Results may differ from a plain program's by a relative error of at most 0.0003.
Values may be sent and summed in bfloat16 or wider, within the bound.
No kernel may reach another device: no remote copies, remote signals or barrier semaphores. Data moves between devices by JAX's collectives and lax.ppermute only.
A program may use at most 128 MiB of HBM per device.

v0:
```python
import jax
import jax.numpy as jnp
from jax import lax
from jax.sharding import PartitionSpec as P

MOMENT_DECAY = 0.9
STAT_DECAY = 0.9
ADAM_EPS = 1e-08
NORM_EPS = 1e-06


def highest(form, left, right):
    return jnp.einsum(
        form, left, right, precision=lax.Precision.HIGHEST, preferred_element_type=jnp.float32
    )


def ratios(adam_square, shampoo_square, entries):
    return jnp.sqrt(adam_square / entries + NORM_EPS) / jnp.sqrt(
        shampoo_square / entries + NORM_EPS
    )


def local(grad_partials, second_moment, left_root, right_root, left_stat, right_stat):
    partials = grad_partials[0]
    block_size = partials.shape[2]
    entries = float(block_size * block_size)
    regrouped = lax.all_to_all(partials, "mp", split_axis=0, concat_axis=1, tiled=True)
    gradient = lax.psum_scatter(
        regrouped.astype(jnp.float32), "dp", scatter_dimension=2, tiled=True
    )
    moment_new = MOMENT_DECAY * second_moment + (1.0 - MOMENT_DECAY) * gradient * gradient
    adam_dir = gradient / (jnp.sqrt(moment_new) + ADAM_EPS)
    whole_grad = lax.all_gather(gradient, "dp", axis=2, tiled=True)
    slab_rows = left_root.shape[1]
    first_row = lax.axis_index("dp") * slab_rows
    grad_rows = lax.dynamic_slice_in_dim(whole_grad, first_row, slab_rows, 1)
    left_new = STAT_DECAY * left_stat + (1.0 - STAT_DECAY) / block_size * highest(
        "bic,bjc->bij", grad_rows, whole_grad
    )
    right_new = STAT_DECAY * right_stat + (1.0 - STAT_DECAY) / block_size * highest(
        "bri,brj->bij", whole_grad, gradient
    )
    product = highest("bij,bjc->bic", left_root, whole_grad)
    shampoo = highest("bic,bcj->bij", lax.all_gather(product, "dp", axis=1, tiled=True), right_root)
    squares = (jnp.sum(adam_dir * adam_dir, axis=(1, 2)), jnp.sum(shampoo * shampoo, axis=(1, 2)))
    adam_square, shampoo_square = lax.psum((squares[0], squares[1]), "dp")
    graft_ratio = ratios(adam_square, shampoo_square, entries)
    update = lax.all_to_all(
        shampoo * graft_ratio[:, None, None], "mp", split_axis=1, concat_axis=0, tiled=True
    )
    return (update, moment_new, left_new, right_new)


def solution(mesh):
    return jax.shard_map(
        local,
        mesh=mesh,
        in_specs=(
            P("dp", None, "mp", None),
            P("mp", None, "dp"),
            P("mp", "dp", None),
            P("mp", None, "dp"),
            P("mp", "dp", None),
            P("mp", None, "dp"),
        ),
        out_specs=(
            P(None, "mp", "dp"),
            P("mp", None, "dp"),
            P("mp", "dp", None),
            P("mp", None, "dp"),
        ),
        check_vma=False,
    )
```

profile of v0, /device:TPU:6, one launch (start us, length us, event | category | flops | bytes accessed | tf_op | source)
XLA Modules:
  0.0 307.8 jit_solution(13249125380026861405)
XLA Ops:
  7.2 0.0 copy-start
  7.2 0.0 reduce-scatter.2.cloned.1.call-start
  7.2 39.8 %all_to_all.21 = bf16[64,16,1024]{2,1,0:T(8,128)(2,1)S(1)} all-to-all(bf16[64,16,1024]{2,1,0:T(8,128)(2,1)} %bitcast.46), channel_id=1, replica_groups=mesh['dp'=2,'mp'=64] {'mp'}, dimensions={0} | all-to-all | bytes 4194304 | tf_op jit(solution)/shard_map/all_to_all | solution.py:28
  47.1 2.4 bitcast_convert_fusion
  49.5 0.0 reduce-scatter.2.cloned.1.call-update
  49.5 0.0 all-gather.4.cloned.1.call-start
  49.6 54.7 %reduce-scatter.2.cloned.1.call-done = f32[1,1024,512]{2,1,0:T(8,128)} async-done(((f32[1,1024,1024]{2,1,0:T(8,128)}), f32[1,1024,512]{2,1,0:T(8,128)}) %reduce-scatter.2.cloned.1.call-update) | async-done | bytes 2097168 | tf_op jit(solution)/shard_map/reduce_scatter | solution.py:29
  104.2 0.0 all-gather.4.cloned.1.call-update
  104.3 0.0 all-gather.6.cloned.1.call-start
  104.3 61.9 %all-gather.4.cloned.1.call-done = f32[1,1024,1024]{2,1,0:T(8,128)} async-done(((f32[1,1024,512]{2,1,0:T(8,128)}), f32[1,1024,1024]{2,1,0:T(8,128)}) %all-gather.4.cloned.1.call-update) | async-done | bytes 4194320 | tf_op jit(solution)/shard_map/all_gather | solution.py:34
  166.2 10.2 %fusion.4 = f32[512,1024]{1,0:T(8,128)} fusion(f32[1,1024,1024]{2,1,0:T(8,128)} %all-gather.4.cloned.1.call-done, f32[1,512,1024]{2,1,0:T(8,128)} %param.8), kind=kOutput, calls=%fused_computation.4 | convolution fusion | flops 6442450944 | bytes 8388608 | tf_op jit(solution)/shard_map/bij,bjc->bic/dot_general | solution.py:13
  176.5 0.0 all-gather.6.cloned.1.call-update
  176.5 5.2 %multiply_reduce_fusion.1 = (f32[]{:T(128)}, f32[1,1024,512]{2,1,0:T(8,128)}) fusion(f32[1,1024,512]{2,1,0:T(8,128)} %reduce-scatter.2.cloned.1.call-done, f32[1,1024,512]{2,1,0:T(8,128)} %param.7), kind=kLoop, calls=%fused_computation.19 | loop fusion | flops 4194303 | bytes 6291460 | tf_op jit(solution)/shard_map/reduce_sum | solution.py:46
  181.7 55.2 %all-gather.6.cloned.1.call-done = f32[1024,1024]{1,0:T(8,128)} async-done(((f32[512,1024]{1,0:T(8,128)}), f32[1024,1024]{1,0:T(8,128)}) %all-gather.6.cloned.1.call-update) | async-done | bytes 4194320 | tf_op jit(solution)/shard_map/all_gather | solution.py:45
  236.9 0.0 copy-done
  236.9 10.3 %multiply_reduce_fusion = (f32[]{:T(128)}, f32[1024,512]{1,0:T(8,128)}) fusion(f32[1024,1024]{1,0:T(8,128)} %all-gather.6.cloned.1.call-done, f32[1,1024,512]{2,1,0:T(8,128)S(1)} %copy-done), kind=kOutput, calls=%fused_computation.18 | convolution fusion | flops 6443499520 | bytes 8388612 | tf_op jit(solution)/shard_map/bic,bcj->bij/dot_general | solution.py:13
  247.2 5.6 %all-reduce = (f32[1]{0:T(128)}, f32[1]{0:T(128)}) all-reduce(f32[1]{0:T(128)} %bitcast.5, f32[1]{0:T(128)} %bitcast.6), channel_id=1, replica_groups=mesh['dp'=2,'mp'=64] {'dp'}, use_global_device_ids=true, to_apply=%region_2.0 | all-reduce | flops 2 | bytes 16 | tf_op jit(solution)/shard_map/psum | solution.py:47
  254.1 1.8 multiply_bitcast_fusion
  255.9 3.5 %copy.10 = f32[1,1024,512]{2,0,1:T(1,128)} copy(f32[1,1024,512]{2,1,0:T(8,128)S(1)} %multiply_bitcast_fusion) | data formatting | bytes 4194304 | tf_op jit(solution)/shard_map/mul | solution.py:50
  259.4 10.6 %all-to-all-start.1 = ((f32[1,1024,512]{2,0,1:T(1,128)}), f32[1,1024,512]{2,0,1:T(1,128)}, u32[]{:S(2)}, u32[]{:S(2)}) async-start(f32[1,1024,512]{2,0,1:T(1,128)} %copy.10), calls=%async_computation.2 | async-start | bytes 4194304 | tf_op jit(solution)/shard_map/all_to_all | solution.py:49
  270.0 0.0 copy-start.1
  270.0 0.0 copy-start.2
  270.0 0.0 copy-start.3
  270.0 10.8 %bitcast_add_fusion.1 = f32[1,512,1024]{2,1,0:T(8,128)} fusion(f32[1,512,1024]{2,1,0:T(8,128)} %param.10, f32[1,1024,1024]{2,1,0:T(8,128)} %all-gather.4.cloned.1.call-done, s32[]{:T(128)S(6)} %select_n.3), kind=kOutput, calls=%fused_computation.11 | convolution fusion | flops 6444023808 | bytes 10485764 | tf_op jit(solution)/shard_map/bic,bjc->bij/dot_general | solution.py:13
  280.9 0.0 copy-done.1
  280.9 0.0 copy-done.2
  280.9 0.0 copy-done.3
  280.9 8.3 %bitcast_add_fusion = f32[1,1024,512]{2,1,0:T(8,128)} fusion(f32[1,1024,512]{2,1,0:T(8,128)S(1)} %copy-done.3, f32[1,1024,512]{2,1,0:T(8,128)S(1)} %copy-done.2, f32[1,1024,1024]{2,1,0:T(8,128)S(1)} %copy-done.1), kind=kOutput, calls=%fused_computation.9 | convolution fusion | flops 6444023808 | bytes 10485760 | tf_op jit(solution)/shard_map/bri,brj->bij/dot_general | solution.py:13
  289.1 9.0 %all-to-all-done.1 = f32[1,1024,512]{2,0,1:T(1,128)} async-done(((f32[1,1024,512]{2,0,1:T(1,128)}), f32[1,1024,512]{2,0,1:T(1,128)}, u32[]{:S(2)}, u32[]{:S(2)}) %all-to-all-start.1) | async-done | bytes 2097184 | tf_op jit(solution)/shard_map/all_to_all | solution.py:49
  298.2 3.1 %copy.11 = f32[1,1024,512]{2,1,0:T(8,128)} copy(f32[1,1024,512]{2,0,1:T(1,128)} %all-to-all-done.1) | data formatting | bytes 4194304
Async XLA Ops:
  7.2 229.7 %copy-start = (f32[1,1024,512]{2,1,0:T(8,128)S(1)}, f32[1,1024,512]{2,1,0:T(8,128)}, u32[]{:S(2)}) copy-start(f32[1,1024,512]{2,1,0:T(8,128)} %param.9) | copy-start | bytes 6291460
  7.2 97.1 %reduce-scatter.2.cloned.1.call-start = ((), (), s32[]{:S(2)}) async-start(), calls=%async_computation.3 | async-start | bytes 6291456 | tf_op jit(solution)/shard_map/reduce_scatter | solution.py:29
  49.5 116.7 %all-gather.4.cloned.1.call-start = ((), (), s32[]{:S(2)}) async-start(), calls=%async_computation.4 | async-start | bytes 6291456 | tf_op jit(solution)/shard_map/all_gather | solution.py:34
  104.3 132.6 %all-gather.6.cloned.1.call-start = ((), (), s32[]{:S(2)}) async-start(), calls=%async_computation.5 | async-start | bytes 6291456 | tf_op jit(solution)/shard_map/all_gather | solution.py:45
  259.4 38.7 %all-to-all-start.1 = ((f32[1,1024,512]{2,0,1:T(1,128)}), f32[1,1024,512]{2,0,1:T(1,128)}, u32[]{:S(2)}, u32[]{:S(2)}) async-start(f32[1,1024,512]{2,0,1:T(1,128)} %copy.10), calls=%async_computation.2 | async-start | bytes 4194304 | tf_op jit(solution)/shard_map/all_to_all | solution.py:49
  270.0 10.8 %copy-start.1 = (f32[1,1024,1024]{2,1,0:T(8,128)S(1)}, f32[1,1024,1024]{2,1,0:T(8,128)}, u32[]{:S(2)}) copy-start(f32[1,1024,1024]{2,1,0:T(8,128)} %all-gather.4.cloned.1.call-done) | copy-start | bytes 12582916
  270.0 10.8 %copy-start.2 = (f32[1,1024,512]{2,1,0:T(8,128)S(1)}, f32[1,1024,512]{2,1,0:T(8,128)}, u32[]{:S(2)}) copy-start(f32[1,1024,512]{2,1,0:T(8,128)} %reduce-scatter.2.cloned.1.call-done) | copy-start | bytes 6291460
  270.0 10.8 %copy-start.3 = (f32[1,1024,512]{2,1,0:T(8,128)S(1)}, f32[1,1024,512]{2,1,0:T(8,128)}, u32[]{:S(2)}) copy-start(f32[1,1024,512]{2,1,0:T(8,128)} %param.11) | copy-start | bytes 6291460
Sparse Core Ops, SparseCore 0:
  49.6 54.5 reduce-scatter.1
  106.0 60.2 all-gather.3
  176.6 60.2 all-gather.5
where the time goes:
time: 312 us; the launch traced here: 308 us
  waiting for transfers between devices  181 us (58%)
  blocking collectives  45.4 us (15%)
  matrix products  39.6 us (13%)
  between operations  15.2 us (5%)
  starting transfers between devices  10.7 us (3%)
  other arithmetic  9.44 us (3%)
  local copies, waits for them, and re-layouts  6.58 us (2%)
    all_gather x1, waiting for transfers between devices, local(): whole_grad = lax.all_gather(gradient, 'dp', axis=2, tiled=True)  61.9 us
    all_gather x1, waiting for transfers between devices, local(): lax.all_gather(product, 'dp', axis=1, tiled=True)  55.2 us
    reduce_scatter x1, waiting for transfers between devices, local(): lax.psum_scatter(regrouped.astype(jnp.float32), 'dp', scatter_dimension=2...  54.7 us
    all_to_all x1, blocking collectives, local(): lax.all_to_all(partials, 'mp', split_axis=0, concat_axis=1, tiled=True)  39.8 us
    dot_general x4, matrix products, highest(): jnp.einsum(form, left, right, precision=lax.Precision.HIGHEST, preferred_...  39.6 us
    all_to_all x1, starting transfers between devices, local(): lax.all_to_all(shampoo * graft_ratio[:, None, None], 'mp', split_axis=1,...  10.6 us
    all_to_all x1, waiting for transfers between devices, local(): lax.all_to_all(shampoo * graft_ratio[:, None, None], 'mp', split_axis=1,...  9.03 us
  transfers between devices with their start and end apart: 4, of which 4 were waited for; matrix products, arithmetic and copies ran while one was open for 8% of the time, Pallas kernels for 0%

commit v1 on v0

v1 whole, which is shorter than its diff:
```python
import jax
import jax.numpy as jnp
from jax import lax
from jax.experimental import pallas as pl
from jax.experimental.pallas import tpu as pltpu
from jax.sharding import PartitionSpec as P

MOMENT_DECAY = 0.9
STAT_DECAY = 0.9
ADAM_EPS = 1e-08
NORM_EPS = 1e-06
SWAP = [(0, 1), (1, 0)]
TAIL = 16
LANES = 128
POWER = 14
SMALLEST = 1e-30
CHUNKS = 4
EARLY = 9 / 16
F32, BF16 = jnp.float32, jnp.bfloat16


VMEM = pl.BlockSpec(memory_space=pltpu.VMEM)
SMEM = pl.BlockSpec(memory_space=pltpu.SMEM)
ANY = pl.BlockSpec(memory_space=pl.ANY)
HBM = pl.BlockSpec(memory_space=pltpu.HBM)


def params(mebibytes):
    return pltpu.CompilerParams(vmem_limit_bytes=mebibytes * 1024 * 1024)


def near(values):
    return pltpu.with_memory_space_constraint(values, pltpu.VMEM)


def far(values):
    return pltpu.with_memory_space_constraint(values, pltpu.HBM)


def exponent_of(top):
    return jnp.floor(jnp.log2(jnp.maximum(top, SMALLEST))) - 8.0


def encode(scaled):
    square = scaled * scaled
    fourth = square * square
    return (fourth * fourth * fourth * (scaled * jnp.abs(scaled))).astype(BF16)


def decode(coded):
    wide = coded.astype(F32)
    size = jnp.abs(wide)
    root = jnp.exp2(jnp.log2(jnp.maximum(size, 1e-37)) * (1.0 / POWER))
    return jnp.where(size == 0.0, 0.0, jnp.where(wide < 0.0, -root, root))


def split(values):
    high = values.astype(BF16)
    return high, (values - high.astype(F32)).astype(BF16)


def dot3(left, right):
    dot = lambda a, b: jnp.dot(a, b, preferred_element_type=F32)
    return dot(left[0], right[0]) + (dot(left[0], right[1]) + dot(left[1], right[0]))


def fold(values):
    rows, columns = values.shape
    return jnp.sum(values.reshape(rows // 8, 8, columns), axis=0)


def parts_of(rows):
    early = int(rows * EARLY) // 32 * 32
    return ((0, early // 2), (early // 2, early)), ((early, (early + rows) // 2), ((early + rows) // 2, rows))


def pack_kernel(group, left_ref, code_ref, left, sems):
    columns = left.shape[1]
    origin = group[0][0]
    fetches = []
    for start, stop in group:
        here = pl.ds(start - origin, stop - start)
        source = left_ref.at[pl.ds(start, stop - start)]
        fetches.append(pltpu.make_async_copy(source, left.at[here], sems.at[len(fetches)]))
        fetches[-1].start()
    tails = []
    for start, stop in group:
        here = slice(start - origin, stop - origin)
        fetches.pop(0).wait()
        values = left[here]
        exponent = exponent_of(jnp.max(jnp.abs(values), axis=(0, 1), keepdims=True))
        code_ref[here] = encode(values * jnp.exp2(-exponent))
        tails.append(jnp.broadcast_to(exponent, (TAIL, columns // 2)))
    code_ref[left.shape[0] :] = jnp.concatenate(tails, axis=1).astype(BF16)


def pack(left, which):
    columns = left.shape[1]
    group = parts_of(left.shape[0])[which]
    depth = group[1][1] - group[0][0]

    def kernel(*refs):
        pack_kernel(group, *refs)

    return pl.pallas_call(
        kernel,
        in_specs=[HBM],
        out_specs=VMEM,
        out_shape=jax.ShapeDtypeStruct((depth + TAIL, columns), BF16),
        scratch_shapes=[pltpu.VMEM((depth, columns), F32), pltpu.SemaphoreType.DMA((2,))],
        compiler_params=params(16),
    )(far(left))


def root_of(code_ref, group):
    origin, end = group[0][0], group[1][1]
    depth = end - origin
    columns = code_ref.shape[1]
    scales = jnp.exp2(code_ref[depth : depth + TAIL].astype(F32)[0:1])
    rows = []
    for part, (start, stop) in enumerate(group):
        lane = part * (columns // 2)
        rows.append(decode(code_ref[start - origin : stop - origin]) * scales[:, lane : lane + 1])
    return jnp.concatenate(rows, axis=0)


def double_kernel(partials_ref, doubled_ref, partials, turned, fetch_sems, write_sems):
    parts = fetch_sems.shape[0]
    blocks = partials.shape[0]
    per = blocks // parts
    fetches, writes = [], []
    for part in range(parts):
        here = pl.ds(part * per, per)
        fetches.append(pltpu.make_async_copy(partials_ref.at[here], partials.at[here], fetch_sems.at[part]))
        fetches[-1].start()
    for part in range(parts):
        fetches[part].wait()
        for block in range(part * per, (part + 1) * per):
            turned[blocks - 1 - block] = partials[block]
        there = pl.ds(blocks - (part + 1) * per, per)
        for copy in range(2):
            writes.append(
                pltpu.make_async_copy(
                    turned.at[there], doubled_ref.at[there, copy], write_sems.at[2 * part + copy]
                )
            )
            writes[-1].start()
    for write in writes:
        write.wait()


def double(partials):
    blocks, slab, size = partials.shape
    return pl.pallas_call(
        double_kernel,
        in_specs=[HBM],
        out_specs=HBM,
        out_shape=pltpu.HBM((blocks, 2, slab, size), BF16),
        scratch_shapes=[
            pltpu.VMEM(partials.shape, BF16),
            pltpu.VMEM(partials.shape, BF16),
            pltpu.SemaphoreType.DMA((4,)),
            pltpu.SemaphoreType.DMA((8,)),
        ],
        compiler_params=params(16),
    )(far(partials))


def coded(shampoo, slab, sent, facts, first):
    rows, half = shampoo.shape
    messages = rows // slab
    grouped = shampoo.reshape(messages, slab, half)
    exponent = exponent_of(jnp.max(jnp.abs(grouped), axis=(1, 2), keepdims=True))
    code = encode(grouped * jnp.exp2(-exponent))
    wide = jnp.broadcast_to(exponent, (messages, TAIL, LANES)).astype(BF16)
    for message in range(messages):
        place = first + (messages - 1 - message)
        for tile in range(half // LANES):
            sent[place, tile * slab : (tile + 1) * slab, :] = code[
                message, :, tile * LANES : (tile + 1) * LANES
            ]
        facts[place] = wide[message]
    return fold(shampoo * shampoo)


def main_kernel(
    side_ref, right_ref, pieces_ref, moment_ref, left_ref, code_ref,
    grad_ref, new_ref, sent, turn_hi, turn_lo, facts_ref, sums_ref,
    pieces, moment, left, grad, new, right_hi, right_lo, fetch_sems, write_sems,
):
    side = side_ref[0]
    blocks, _, slab, size = pieces.shape
    half = size // 2
    chunks = CHUNKS
    rows = size // chunks
    messages = rows // slab
    early = parts_of(half)[0]

    def fetch(source, target, slot):
        copy = pltpu.make_async_copy(source, target, fetch_sems.at[slot])
        copy.start()
        return copy

    def fetch_pieces(chunk):
        here = pl.ds(blocks - (chunk + 1) * messages, messages)
        return fetch(pieces_ref.at[here], pieces.at[here], chunk)

    def fetch_moment(chunk):
        here = pl.ds(chunk * rows, rows)
        return fetch(moment_ref.at[here], moment.at[here], chunks + chunk)

    piece_arrivals = [fetch_pieces(chunk) for chunk in range(chunks)]
    moment_arrivals = [fetch_moment(chunk) for chunk in range(chunks)]
    writes = []

    def write(source, target):
        writes.append(pltpu.make_async_copy(source, target, write_sems.at[len(writes)]))
        writes[-1].start()

    right_hi[...], right_lo[...] = split(right_ref[...])
    adam = jnp.zeros((8, half), F32)
    for chunk in range(chunks):
        here = slice(chunk * rows, (chunk + 1) * rows)
        piece_arrivals[chunk].wait()
        if chunk == 0:
            left_arrival = fetch(left_ref, left, 2 * chunks)
        for message in range(messages):
            source = chunk * messages + message
            piece = blocks - 1 - source
            grad[source * slab : (source + 1) * slab] = pieces[piece, 0].astype(F32) + pieces[
                piece, 1
            ].astype(F32)
        write(grad.at[pl.ds(chunk * rows, rows)], grad_ref.at[pl.ds(chunk * rows, rows)])
        turned = dot3(split(grad[here]), (right_hi[...], right_lo[...]))
        turn_hi[here], turn_lo[here] = split(turned)
        mine = grad[here, pl.ds(pl.multiple_of(side * half, half), half)]
        moment_arrivals[chunk].wait()
        moment_new = MOMENT_DECAY * moment[here] + (1.0 - MOMENT_DECAY) * mine * mine
        new[here] = moment_new
        direction = mine / (jnp.sqrt(moment_new) + ADAM_EPS)
        adam += fold(direction * direction)
    write(new, new_ref)

    def finish(left, row_block):
        shampoo = dot3(split(left), (turn_hi[...], turn_lo[...]))
        count = left.shape[0] // slab
        first = blocks - count - row_block
        return coded(shampoo, slab, sent, facts_ref, first)

    squares = jnp.zeros((8, half), F32)
    left_arrival.wait()
    for start in range(0, half, rows):
        squares += finish(left[start : start + rows], side * (blocks // 2) + start // slab)
    squares += finish(root_of(code_ref, early), (1 - side) * (blocks // 2))
    sums_ref[:8] = adam
    sums_ref[8:] = squares
    for copy in writes:
        copy.wait()


def main(side, pieces, moment, right, left, code):
    size, half = right.shape
    blocks, _, slab, _ = pieces.shape
    data = half // LANES * slab
    return pl.pallas_call(
        main_kernel,
        in_specs=[SMEM, VMEM, HBM, HBM, HBM, VMEM],
        out_specs=[HBM, ANY, VMEM, VMEM, VMEM, VMEM, VMEM],
        out_shape=[
            pltpu.HBM((size, size), F32),
            jax.ShapeDtypeStruct((size, half), F32),
            pltpu.VMEM((blocks, data, LANES), BF16),
            pltpu.VMEM((size, half), BF16),
            pltpu.VMEM((size, half), BF16),
            pltpu.VMEM((blocks, TAIL, LANES), BF16),
            pltpu.VMEM((16, half), F32),
        ],
        scratch_shapes=[
            pltpu.VMEM(pieces.shape, BF16),
            pltpu.VMEM(moment.shape, F32),
            pltpu.VMEM(left.shape, F32),
            pltpu.VMEM((size, size), F32),
            pltpu.VMEM(moment.shape, F32),
            pltpu.VMEM((size, half), BF16),
            pltpu.VMEM((size, half), BF16),
            pltpu.SemaphoreType.DMA((2 * CHUNKS + 1,)),
            pltpu.SemaphoreType.DMA((CHUNKS + 1,)),
        ],
        compiler_params=params(36),
        cost_estimate=pl.CostEstimate(
            flops=12 * size * size * half, bytes_accessed=16 * size * size, transcendentals=4 * size * half
        ),
    )(side, near(right), far(pieces), far(moment), far(left), near(code))


def last_kernel(side_ref, turn_hi, turn_lo, code_ref, facts_ref, sums_ref, done_ref, sent_ref, sent, facts, sems):
    side = side_ref[0]
    blocks = facts.shape[0]
    slab = 16
    data = sent.shape[1]
    half = turn_hi.shape[1]
    late = parts_of(half)[1]
    count = sent.shape[0]
    row_block = (1 - side) * (blocks // 2) + late[0][0] // slab
    first = blocks - count - row_block

    writes = []

    def write(source, target):
        writes.append(pltpu.make_async_copy(source, target, sems.at[len(writes)]))
        writes[-1].start()

    rest = blocks // 2 - count
    for start, extent in (((1 - side) * (blocks // 2), blocks // 2), (first + count, rest)):
        here = pl.ds(start, extent)
        write(done_ref.at[here], sent_ref.at[here, pl.ds(0, data)])
    facts[...] = facts_ref[...]
    shampoo = dot3(split(root_of(code_ref, late)), (turn_hi[...], turn_lo[...]))
    squares = coded(shampoo, slab, sent, facts.at[pl.ds(first, count)], 0)
    write(sent, sent_ref.at[pl.ds(first, count), pl.ds(0, data)])

    values = facts[...]
    lane = lax.broadcasted_iota(jnp.int32, values.shape, 2)
    place = 1
    for total in (sums_ref[:8], sums_ref[8:] + squares):
        rest = jnp.sum(total, axis=(0, 1), keepdims=True)
        for _ in range(3):
            piece = rest.astype(BF16)
            rest = rest - piece.astype(F32)
            values = jnp.where(lane == place, piece.reshape(1, 1, 1), values)
            place += 1
    facts[...] = values
    write(facts, sent_ref.at[:, pl.ds(data, TAIL)])
    for copy in writes:
        copy.wait()


def last(side, turn_hi, turn_lo, code, facts, sums, done):
    size, half = turn_hi.shape
    blocks, data, lanes = done.shape
    (start, _), (_, stop) = parts_of(half)[1]
    return pl.pallas_call(
        last_kernel,
        in_specs=[SMEM] + [VMEM] * 6,
        out_specs=HBM,
        out_shape=pltpu.HBM((blocks, data + TAIL, lanes), BF16),
        scratch_shapes=[
            pltpu.VMEM(((stop - start) // 16, data, LANES), BF16),
            pltpu.VMEM(facts.shape, BF16),
            pltpu.SemaphoreType.DMA((4,)),
        ],
        compiler_params=params(16),
        cost_estimate=pl.CostEstimate(
            flops=6 * size * half * (stop - start), bytes_accessed=8 * size * half, transcendentals=0
        ),
    )(side, near(turn_hi), near(turn_lo), near(code), near(facts), near(sums), near(done))


def facts_kernel(got_ref, o_ref):
    depth = got_ref.shape[1]
    o_ref[...] = got_ref[:, depth - TAIL :, :].astype(F32)[:, 0, :]


def facts_of(got):
    blocks, _, lanes = got.shape
    return pl.pallas_call(
        facts_kernel,
        in_specs=[VMEM],
        out_specs=VMEM,
        out_shape=pltpu.VMEM((blocks, lanes), F32),
        compiler_params=params(16),
    )(near(got))


def unpack_kernel(got_ref, o_ref):
    blocks, slab, columns = o_ref.shape
    for tile in range(columns // LANES):
        values = decode(got_ref[:, tile * slab : (tile + 1) * slab, :])
        for block in range(blocks):
            o_ref[block, :, tile * LANES : (tile + 1) * LANES] = values[blocks - 1 - block]


def unpack(got, slab):
    blocks, depth, lanes = got.shape
    return pl.pallas_call(
        unpack_kernel,
        in_specs=[VMEM],
        out_specs=VMEM,
        out_shape=pltpu.VMEM((blocks, slab, (depth - TAIL) // slab * lanes), F32),
        compiler_params=params(16),
        cost_estimate=pl.CostEstimate(
            flops=20 * blocks * depth * lanes, bytes_accessed=8 * blocks * depth * lanes, transcendentals=0
        ),
    )(near(got))


def scale_kernel(entries, values_ref, mine_ref, other_ref, o_ref, scaled, sems):
    blocks = values_ref.shape[0]
    mine = mine_ref[...]
    both = mine + other_ref[...]
    total = lambda k: (both[:, k : k + 1] + both[:, k + 1 : k + 2]) + both[:, k + 2 : k + 3]
    ratio = jnp.sqrt(total(1) / entries + NORM_EPS) / jnp.sqrt(total(4) / entries + NORM_EPS)
    factor = ratio * jnp.exp2(mine[:, 0:1])
    parts = sems.shape[0]
    per = blocks // parts
    writes = []
    for part in range(parts):
        for block in range(part * per, (part + 1) * per):
            source = blocks - 1 - block
            scaled[block] = values_ref[block] * factor[source : source + 1]
        here = pl.ds(part * per, per)
        writes.append(pltpu.make_async_copy(scaled.at[here], o_ref.at[here], sems.at[part]))
        writes[-1].start()
    for write in writes:
        write.wait()


def rescale(values, mine, other, entries):
    def kernel(*refs):
        scale_kernel(entries, *refs)

    return pl.pallas_call(
        kernel,
        in_specs=[VMEM] * 3,
        out_specs=ANY,
        out_shape=jax.ShapeDtypeStruct(values.shape, F32),
        scratch_shapes=[pltpu.VMEM(values.shape, F32), pltpu.SemaphoreType.DMA((4,))],
        compiler_params=params(16),
    )(near(values), mine, other)


def highest(form, left, right):
    return jnp.einsum(form, left, right, precision=lax.Precision.HIGH, preferred_element_type=F32)


def local(grad_partials, second_moment, left_root, right_root, left_stat, right_stat):
    partials = grad_partials[0]
    blocks, slab, size = partials.shape
    half = size // 2
    side = lax.axis_index("dp")

    left = left_root[0]
    early = lax.ppermute(pack(left, 0), "dp", SWAP)

    def deliver(values, left):
        pieces = lax.all_to_all(
            double(values).reshape(2 * blocks, slab, size),
            ("mp", "dp"),
            split_axis=0,
            concat_axis=0,
            tiled=True,
            axis_index_groups=[list(range(2 * blocks))[::-1]],
        )
        return pieces, pack(left, 1)

    def nothing(values, left):
        shapes = jax.eval_shape(lambda: (jnp.zeros((2 * blocks, slab, size), values.dtype), pack(left, 1)))
        return tuple(jnp.zeros(each.shape, each.dtype) for each in shapes)

    pieces, late = lax.cond((side + 2) // 2 == 1, deliver, nothing, partials, left)
    pieces = pieces.reshape(blocks, 2, slab, size)
    late = lax.ppermute(late, "dp", SWAP)
    where = side.astype(jnp.int32).reshape(1)
    grad, moment_new, sent, turn_hi, turn_lo, facts, sums = main(
        where, pieces, second_moment[0], right_root[0], left, early
    )
    sent = last(where, turn_hi, turn_lo, late, facts, sums, sent)
    got = lax.all_to_all(
        sent, "mp", split_axis=0, concat_axis=0, tiled=True, axis_index_groups=[list(range(blocks))[::-1]]
    )
    scale = (1.0 - STAT_DECAY) / size
    rows = lax.dynamic_slice_in_dim(grad, side * half, half, 0)
    columns = lax.dynamic_slice_in_dim(grad, side * half, half, 1)
    left_new = STAT_DECAY * left_stat[0] + scale * highest("ic,jc->ij", rows, grad)
    right_new = STAT_DECAY * right_stat[0] + scale * highest("ri,rj->ij", grad, columns)
    got, left_new, right_new = lax.optimization_barrier((got, left_new, right_new))
    mine = facts_of(got)
    other = lax.ppermute(mine, "dp", SWAP)
    update = rescale(unpack(got, slab), mine, other, float(size * size))
    return (update, moment_new[None], left_new[None], right_new[None])


def solution(mesh):
    return jax.shard_map(
        local,
        mesh=mesh,
        in_specs=(
            P("dp", None, "mp", None),
            P("mp", None, "dp"),
            P("mp", "dp", None),
            P("mp", None, "dp"),
            P("mp", "dp", None),
            P("mp", None, "dp"),
        ),
        out_specs=(
            P(None, "mp", "dp"),
            P("mp", None, "dp"),
            P("mp", "dp", None),
            P("mp", None, "dp"),
        ),
        check_vma=False,
    )
```

time: 312 us -> 118 us (0.38); the launches traced: 308 us -> 117 us
  waiting for transfers between devices: 181 us -> 57.4 us
  blocking collectives: 45.4 us -> 0 us
  matrix products: 39.6 us -> 12.8 us
  Pallas kernels: 0 us -> 22.8 us
  between operations: 15.2 us -> 0.87 us
  starting transfers between devices: 10.7 us -> 23.3 us
  other arithmetic: 9.44 us -> 0 us
  local copies, waits for them, and re-layouts: 6.58 us -> 0.02 us
    all_gather x2 -> x0, waiting for transfers between devices: 117 us -> none  [the longest x1 61.9 us: local(): whole_grad = lax.all_gather(gradient, 'dp', axis=2, tiled=True)]
    reduce_scatter x1 -> x0, waiting for transfers between devices: 54.7 us -> none  [local(): lax.psum_scatter(regrouped.astype(jnp.float32), 'dp', scatter_dimension=2...]
    all_to_all x1 -> x2, waiting for transfers between devices: 9.03 us -> 53.5 us  [the longest x1 47.9 us: deliver(): lax.all_to_all(double(values).reshape(2 * blocks, slab, size), ('mp', 'dp...]
    all_to_all x1 -> x0, blocking collectives: 39.8 us -> none  [local(): lax.all_to_all(partials, 'mp', split_axis=0, concat_axis=1, tiled=True)]
    dot_general x4 -> x2, matrix products: 39.6 us -> 12.8 us  [highest(): jnp.einsum(form, left, right, precision=lax.Precision.HIGH, preferred_ele...]
    pallas_call x0 -> x8, Pallas kernels: none -> 22.8 us  [the longest x1 10.2 us: main(): pl.pallas_call(main_kernel, in_specs=[SMEM, VMEM, HBM, HBM, HBM, VMEM], o...]
    all_to_all x1 -> x2, starting transfers between devices: 10.6 us -> 20.5 us  [the longest x1 11.3 us: deliver(): lax.all_to_all(double(values).reshape(2 * blocks, slab, size), ('mp', 'dp...]
    psum x1 -> x0, blocking collectives: 5.56 us -> none  [local(): adam_square, shampoo_square = lax.psum((squares[0], squares[1]), 'dp')]
  transfers between devices with their start and end apart: 4 -> 5, of which waited for: 4 -> 4; matrix products, arithmetic and copies ran while one was open for 8% -> 11% of each run, Pallas kernels for 0% -> 14%
where the time goes in v1:
time: 118 us; the launch traced here: 117 us
  waiting for transfers between devices  57.4 us (49%)
  starting transfers between devices  23.3 us (20%)
  Pallas kernels  22.8 us (19%)
  matrix products  12.8 us (11%)
    all_to_all x1, waiting for transfers between devices, deliver(): lax.all_to_all(double(values).reshape(2 * blocks, slab, size), ('mp', 'dp...  47.9 us
    dot_general x2, matrix products, highest(): jnp.einsum(form, left, right, precision=lax.Precision.HIGH, preferred_ele...  12.8 us
    all_to_all x1, starting transfers between devices, deliver(): lax.all_to_all(double(values).reshape(2 * blocks, slab, size), ('mp', 'dp...  11.3 us
    pallas_call x1, Pallas kernels, main(): pl.pallas_call(main_kernel, in_specs=[SMEM, VMEM, HBM, HBM, HBM, VMEM], o...  10.2 us
    all_to_all x1, starting transfers between devices, local(): lax.all_to_all(sent, 'mp', split_axis=0, concat_axis=0, tiled=True, axis_...  9.23 us
    all_to_all x1, waiting for transfers between devices, local(): lax.all_to_all(sent, 'mp', split_axis=0, concat_axis=0, tiled=True, axis_...  5.59 us
    pallas_call x2, Pallas kernels, pack(): pl.pallas_call(kernel, in_specs=[HBM], out_specs=VMEM, out_shape=jax.Shap...  4.67 us
    pallas_call x1, Pallas kernels, double(): pl.pallas_call(double_kernel, in_specs=[HBM], out_specs=HBM, out_shape=pl...  3.27 us
  transfers between devices with their start and end apart: 5, of which 4 were waited for; matrix products, arithmetic and copies ran while one was open for 11% of the time, Pallas kernels for 14%

profile of v1, /device:TPU:6, one launch (start us, length us, event | category | flops | bytes accessed | tf_op | source)
XLA Modules:
  0.0 117.2 jit_solution(9914599136692490999)
XLA Ops:
  0.6 2.1 %shard_map.94 = bf16[304,1024]{1,0:T(8,128)(2,1)S(1)} custom-call(f32[512,1024]{1,0:T(8,128)} %bitcast.18), custom_call_target="tpu_custom_call" | custom-call | tf_op jit(solution)/shard_map/pallas_call | solution.py:105
  2.7 0.9 collective-permute-start
  3.6 0.0 copy-start
  3.6 65.1 %conditional.1 = (bf16[240,1024]{1,0:T(8,128)(2,1)}, bf16[64,2,16,1024]{3,2,1,0:T(8,128)(2,1)}) conditional(s32[]{:T(128)} %convert_element_type.3, () %tuple.19, (f32[512,1024]{1,0:T(8,128)}, bf16[1,64,16,1024]{3,2,1,0:T(8,128)(2,1)}) %tuple.25), branch_computations={%region_0.1_spmd, %region_1.2_spmd} | conditional | bytes 12582960 | solution.py:460
  3.6 3.3 %branch_1_fun.3 = bf16[64,2,16,1024]{3,2,1,0:T(8,128)(2,1)} custom-call(bf16[64,16,1024]{2,1,0:T(8,128)(2,1)} %bitcast.21), custom_call_target="tpu_custom_call" | custom-call | tf_op jit(solution)/shard_map/cond/branch_1_fun/pallas_call | solution.py:154
  6.9 11.3 %all-to-all-start = ((bf16[128,16,1024]{2,1,0:T(8,128)(2,1)}), bf16[128,16,1024]{2,1,0:T(8,128)(2,1)}, u32[]{:S(2)}, u32[]{:S(2)}) async-start(bf16[128,16,1024]{2,1,0:T(8,128)(2,1)} %bitcast.17), calls=%async_computation | async-start | bytes 8388608 | tf_op jit(solution)/shard_map/cond/branch_1_fun/all_to_all | solution.py:446
  18.2 2.6 %branch_1_fun.2 = bf16[240,1024]{1,0:T(8,128)(2,1)} custom-call(f32[512,1024]{1,0:T(8,128)} %get-tuple-element.6.refs_0_), custom_call_target="tpu_custom_call" | custom-call | tf_op jit(solution)/shard_map/cond/branch_1_fun/pallas_call | solution.py:105
  20.8 47.9 %all-to-all-done = bf16[128,16,1024]{2,1,0:T(8,128)(2,1)} async-done(((bf16[128,16,1024]{2,1,0:T(8,128)(2,1)}), bf16[128,16,1024]{2,1,0:T(8,128)(2,1)}, u32[]{:S(2)}, u32[]{:S(2)}) %all-to-all-start) | async-done | bytes 4194336 | tf_op jit(solution)/shard_map/cond/branch_1_fun/all_to_all | solution.py:446
  68.7 1.2 %collective-permute-start.1 = (bf16[240,1024]{1,0:T(8,128)(2,1)}, bf16[240,1024]{1,0:T(8,128)(2,1)S(1)}, u32[]{:S(2)}, u32[]{:S(2)}) collective-permute-start(bf16[240,1024]{1,0:T(8,128)(2,1)} %get-tuple-element.27), channel_id=1, source_target_pairs={{0,64},{64,0},{1,65},{65,1},{2,66},{66,2},{3,67},{67,3},{4,68},{68... | collective-permute-start | bytes 1474568 | tf_op jit(solution)/shard_map/ppermute | solution.py:462
  69.9 0.0 collective-permute-done.code_ref
  69.9 0.0 copy-done
  69.9 10.2 %shard_map.95 = (f32[1024,1024]{1,0:T(8,128)}, f32[1024,512]{1,0:T(8,128)}, bf16[64,64,128]{2,1,0:T(8,128)(2,1)S(1)}, bf16[1024,512]{1,0:T(8,128)(2,1)S(1)}, bf1...) custom-call(s32[1]{0:T(128)} %bitcast.3.side_ref, f32[1024,512]{1,0:T(8,128)S(1)} %bitcast.16, ...), custom_call_target="tpu_custom_call" | custom-call | flops 6442450944 | bytes 16777216 | tf_op jit(solution)/shard_map/pallas_call | solution.py:265
  80.1 1.4 %collective-permute-done.1.code_ref = bf16[240,1024]{1,0:T(8,128)(2,1)S(1)} collective-permute-done((bf16[240,1024]{1,0:T(8,128)(2,1)}, bf16[240,1024]{1,0:T(8,128)(2,1)S(1)}, u32[]{:S(2)}, u32[]{:S(2)}) %collective-permute-start.1) | collective-permute-done | bytes 491552 | tf_op jit(solution)/shard_map/ppermute | solution.py:462
  81.5 2.2 %shard_map.96 = bf16[64,80,128]{2,1,0:T(8,128)(2,1)} custom-call(s32[1]{0:T(128)} %bitcast.3.side_ref, bf16[1024,512]{1,0:T(8,128)(2,1)S(1)} %get-tuple-element.25.turn_hi, bf16[1024,512]{1,0:T(8,128)(2,1)S(1)} %get-tuple-element.26.turn_lo, bf16[240,1024]{1,0:T(8,128)(2,1)S(1)} %collective-permute-done.1.code_ref, ...), custom_call_target="tpu_custom_call" | custom-call | flops 704643072 | bytes 4194304 | tf_op jit(solution)/shard_map/pallas_call | solution.py:342
  83.7 0.0 copy-start.2
  83.7 9.2 %all-to-all-start.1 = ((bf16[64,80,128]{2,1,0:T(8,128)(2,1)}), bf16[64,80,128]{2,1,0:T(8,128)(2,1)S(1)}, u32[]{:S(2)}, u32[]{:S(2)}) async-start(bf16[64,80,128]{2,1,0:T(8,128)(2,1)} %shard_map.96), calls=%async_computation.1 | async-start | bytes 2621440 | tf_op jit(solution)/shard_map/all_to_all | solution.py:468
  93.0 0.0 copy-done.2
  93.0 0.0 copy-start.1
  93.0 0.0 copy-start.3
  93.0 7.9 %bitcast_add_fusion = f32[1024,512]{1,0:T(8,128)} fusion(f32[1,1024,512]{2,1,0:T(8,128)S(1)} %copy-done.2, f32[1024,1024]{1,0:T(8,128)} %get-tuple-element.31, s32[]{:T(128)S(6)} %select_n.10), kind=kOutput, calls=%fused_computation | convolution fusion | flops 3222798336 | bytes 10485764 | tf_op jit(solution)/shard_map/ri,rj->ij/dot_general | solution.py:433
  100.9 0.0 copy-done.1
  100.9 0.0 copy-done.3
  100.9 4.9 %bitcast_add_fusion.1 = f32[512,1024]{1,0:T(8,128)} fusion(f32[1,512,1024]{2,1,0:T(8,128)S(1)} %copy-done.3, f32[1024,1024]{1,0:T(8,128)S(1)} %copy-done.1, s32[]{:T(128)S(6)} %select_n.10), kind=kOutput, calls=%fused_computation.1 | convolution fusion | flops 3222798336 | bytes 10485764 | tf_op jit(solution)/shard_map/ic,jc->ij/dot_general | solution.py:433
  105.8 5.6 %all-to-all-done.1.got_ref = bf16[64,80,128]{2,1,0:T(8,128)(2,1)S(1)} async-done(((bf16[64,80,128]{2,1,0:T(8,128)(2,1)}), bf16[64,80,128]{2,1,0:T(8,128)(2,1)S(1)}, u32[]{:S(2)}, u32[]{:S(2)}) %all-to-all-start.1) | async-done | bytes 1310752 | tf_op jit(solution)/shard_map/all_to_all | solution.py:468
  111.4 0.7 collective-permute-start.2
  112.1 0.8 shard_map.97.refs_0_
  112.9 2.5 %collective-permute-done.2.refs_2_ = f32[64,128]{1,0:T(8,128)S(1)} collective-permute-done((f32[64,128]{1,0:T(8,128)S(1)}, f32[64,128]{1,0:T(8,128)S(1)}, u32[]{:S(2)}, u32[]{:S(2)}) %collective-permute-start.2) | collective-permute-done | bytes 32800 | tf_op jit(solution)/shard_map/ppermute | solution.py:478
  115.4 1.7 %shard_map.99 = f32[64,16,512]{2,1,0:T(8,128)} custom-call(f32[64,16,512]{2,1,0:T(8,128)S(1)} %shard_map.97.refs_0_, f32[64,128]{1,0:T(8,128)S(1)} %shard_map.98.refs_1_, f32[64,128]{1,0:T(8,128)S(1)} %collective-permute-done.2.refs_2_), custom_call_target="tpu_custom_call" | custom-call | tf_op jit(solution)/shard_map/pallas_call | solution.py:422
  (1 shorter events, 0.0 us)
Async XLA Ops:
  2.7 67.2 %collective-permute-start = (bf16[304,1024]{1,0:T(8,128)(2,1)S(1)}, bf16[304,1024]{1,0:T(8,128)(2,1)S(1)}, u32[]{:S(2)}, u32[]{:S(2)}) collective-permute-start(bf16[304,1024]{1,0:T(8,128)(2,1)S(1)} %shard_map.94), channel_id=1, source_target_pairs={{0,64},{64,0},{1,65},{65,1},{2,66},{66,2},{3,67},{67,3},{4,68},{68... | collective-permute-start | bytes 1867784 | tf_op jit(solution)/shard_map/ppermute | solution.py:443
  3.6 66.3 %copy-start = (f32[1,1024,512]{2,1,0:T(8,128)S(1)}, f32[1,1024,512]{2,1,0:T(8,128)}, u32[]{:S(2)}) copy-start(f32[1,1024,512]{2,1,0:T(8,128)} %param.11) | copy-start | bytes 6291460
  6.9 61.8 %all-to-all-start = ((bf16[128,16,1024]{2,1,0:T(8,128)(2,1)}), bf16[128,16,1024]{2,1,0:T(8,128)(2,1)}, u32[]{:S(2)}, u32[]{:S(2)}) async-start(bf16[128,16,1024]{2,1,0:T(8,128)(2,1)} %bitcast.17), calls=%async_computation | async-start | bytes 8388608 | tf_op jit(solution)/shard_map/cond/branch_1_fun/all_to_all | solution.py:446
  68.7 12.8 %collective-permute-start.1 = (bf16[240,1024]{1,0:T(8,128)(2,1)}, bf16[240,1024]{1,0:T(8,128)(2,1)S(1)}, u32[]{:S(2)}, u32[]{:S(2)}) collective-permute-start(bf16[240,1024]{1,0:T(8,128)(2,1)} %get-tuple-element.27), channel_id=1, source_target_pairs={{0,64},{64,0},{1,65},{65,1},{2,66},{66,2},{3,67},{67,3},{4,68},{68... | collective-permute-start | bytes 1474568 | tf_op jit(solution)/shard_map/ppermute | solution.py:462
  83.7 9.3 %copy-start.2 = (f32[1,1024,512]{2,1,0:T(8,128)S(1)}, f32[1,1024,512]{2,1,0:T(8,128)}, u32[]{:S(2)}) copy-start(f32[1,1024,512]{2,1,0:T(8,128)} %param.13) | copy-start | bytes 6291460
  83.7 27.7 %all-to-all-start.1 = ((bf16[64,80,128]{2,1,0:T(8,128)(2,1)}), bf16[64,80,128]{2,1,0:T(8,128)(2,1)S(1)}, u32[]{:S(2)}, u32[]{:S(2)}) async-start(bf16[64,80,128]{2,1,0:T(8,128)(2,1)} %shard_map.96), calls=%async_computation.1 | async-start | bytes 2621440 | tf_op jit(solution)/shard_map/all_to_all | solution.py:468
  93.0 7.9 %copy-start.1 = (f32[1024,1024]{1,0:T(8,128)S(1)}, f32[1024,1024]{1,0:T(8,128)}, u32[]{:S(2)}) copy-start(f32[1024,1024]{1,0:T(8,128)} %get-tuple-element.31) | copy-start | bytes 12582916
  93.0 7.9 %copy-start.3 = (f32[1,512,1024]{2,1,0:T(8,128)S(1)}, f32[1,512,1024]{2,1,0:T(8,128)}, u32[]{:S(2)}) copy-start(f32[1,512,1024]{2,1,0:T(8,128)} %param.12) | copy-start | bytes 6291460
  111.4 4.0 %collective-permute-start.2 = (f32[64,128]{1,0:T(8,128)S(1)}, f32[64,128]{1,0:T(8,128)S(1)}, u32[]{:S(2)}, u32[]{:S(2)}) collective-permute-start(f32[64,128]{1,0:T(8,128)S(1)} %shard_map.98.refs_1_), channel_id=1, source_target_pairs={{0,64},{64,0},{1,65},{65,1},{2,66},{66,2},{3,67},{67,3},{4,68},{68... | collective-permute-start | bytes 98312 | tf_op jit(solution)/shard_map/ppermute | solution.py:478

commit v2 on v1

--- a/solution.py
+++ b/solution.py
@@ -74,8 +74,8 @@
     return ((0, early // 2), (early // 2, early)), ((early, (early + rows) // 2), ((early + rows) // 2, rows))
 
 
-def pack_kernel(group, left_ref, code_ref, left, sems):
-    columns = left.shape[1]
+def pack_kernel(group, left_ref, code_ref, left, sems, others=()):
+    depth, columns = left.shape
     origin = group[0][0]
     fetches = []
     for start, stop in group:
@@ -83,15 +83,64 @@
         source = left_ref.at[pl.ds(start, stop - start)]
         fetches.append(pltpu.make_async_copy(source, left.at[here], sems.at[len(fetches)]))
         fetches[-1].start()
+    for other in others:
+        other.start()
     tails = []
     for start, stop in group:
         here = slice(start - origin, stop - origin)
         fetches.pop(0).wait()
         values = left[here]
         exponent = exponent_of(jnp.max(jnp.abs(values), axis=(0, 1), keepdims=True))
-        code_ref[here] = encode(values * jnp.exp2(-exponent))
-        tails.append(jnp.broadcast_to(exponent, (TAIL, columns // 2)))
-    code_ref[left.shape[0] :] = jnp.concatenate(tails, axis=1).astype(BF16)
+        code = encode(values * jnp.exp2(-exponent))
+        for tile in range(columns // LANES):
+            first = tile * depth
+            code_ref[first + start - origin : first + stop - origin] = code[
+                :, tile * LANES : (tile + 1) * LANES
+            ]
+        tails.append(jnp.broadcast_to(exponent, (TAIL, LANES)))
+    lane = lax.broadcasted_iota(jnp.int32, (TAIL, LANES), 1)
+    code_ref[columns // LANES * depth :] = jnp.where(lane < LANES // 2, *tails).astype(BF16)
+
+
+def front_kernel(group, left_ref, partials_ref, code_ref, turned_ref, left, partials, sems, partial_sems):
+    parts = partial_sems.shape[0]
+    blocks = partials.shape[0]
+    per = blocks // parts
+    fetches = []
+    for part in range(parts):
+        here = pl.ds(part * per, per)
+        fetches.append(pltpu.make_async_copy(partials_ref.at[here], partials.at[here], partial_sems.at[part]))
+    pack_kernel(group, left_ref, code_ref, left, sems, fetches)
+    for part in range(parts):
+        fetches[part].wait()
+        for block in range(part * per, (part + 1) * per):
+            turned_ref[blocks - 1 - block] = partials[block]
+
+
+def front(left, partials):
+    columns = left.shape[1]
+    group = parts_of(left.shape[0])[0]
+    depth = group[1][1] - group[0][0]
+
+    def kernel(*refs):
+        front_kernel(group, *refs)
+
+    return pl.pallas_call(
+        kernel,
+        in_specs=[HBM, HBM],
+        out_specs=[VMEM, VMEM],
+        out_shape=[
+            jax.ShapeDtypeStruct((columns // LANES * depth + TAIL, LANES), BF16),
+            pltpu.VMEM(partials.shape, BF16),
+        ],
+        scratch_shapes=[
+            pltpu.VMEM((depth, columns), F32),
+            pltpu.VMEM(partials.shape, BF16),
+            pltpu.SemaphoreType.DMA((2,)),
+            pltpu.SemaphoreType.DMA((2,)),
+        ],
+        compiler_params=params(16),
+    )(far(left), far(partials))
 
 
 def pack(left, which):
@@ -106,7 +155,7 @@
         kernel,
         in_specs=[HBM],
         out_specs=VMEM,
-        out_shape=jax.ShapeDtypeStruct((depth + TAIL, columns), BF16),
+        out_shape=jax.ShapeDtypeStruct((columns // LANES * depth + TAIL, LANES), BF16),
         scratch_shapes=[pltpu.VMEM((depth, columns), F32), pltpu.SemaphoreType.DMA((2,))],
         compiler_params=params(16),
     )(far(left))
@@ -115,55 +164,38 @@
 def root_of(code_ref, group):
     origin, end = group[0][0], group[1][1]
     depth = end - origin
-    columns = code_ref.shape[1]
-    scales = jnp.exp2(code_ref[depth : depth + TAIL].astype(F32)[0:1])
+    tiles = (code_ref.shape[0] - TAIL) // depth
+    scales = jnp.exp2(code_ref[tiles * depth :].astype(F32)[0:1])
     rows = []
     for part, (start, stop) in enumerate(group):
-        lane = part * (columns // 2)
-        rows.append(decode(code_ref[start - origin : stop - origin]) * scales[:, lane : lane + 1])
+        lane = part * (LANES // 2)
+        columns = [
+            decode(code_ref[tile * depth + start - origin : tile * depth + stop - origin])
+            for tile in range(tiles)
+        ]
+        rows.append(jnp.concatenate(columns, axis=1) * scales[:, lane : lane + 1])
     return jnp.concatenate(rows, axis=0)
 
 
-def double_kernel(partials_ref, doubled_ref, partials, turned, fetch_sems, write_sems):
-    parts = fetch_sems.shape[0]
-    blocks = partials.shape[0]
-    per = blocks // parts
-    fetches, writes = [], []
-    for part in range(parts):
-        here = pl.ds(part * per, per)
-        fetches.append(pltpu.make_async_copy(partials_ref.at[here], partials.at[here], fetch_sems.at[part]))
-        fetches[-1].start()
-    for part in range(parts):
-        fetches[part].wait()
-        for block in range(part * per, (part + 1) * per):
-            turned[blocks - 1 - block] = partials[block]
-        there = pl.ds(blocks - (part + 1) * per, per)
-        for copy in range(2):
-            writes.append(
-                pltpu.make_async_copy(
-                    turned.at[there], doubled_ref.at[there, copy], write_sems.at[2 * part + copy]
-                )
-            )
-            writes[-1].start()
+def double_kernel(turned_ref, doubled_ref, sems):
+    writes = []
+    for copy in range(2):
+        writes.append(pltpu.make_async_copy(turned_ref, doubled_ref.at[:, copy], sems.at[copy]))
+        writes[-1].start()
     for write in writes:
         write.wait()
 
 
-def double(partials):
-    blocks, slab, size = partials.shape
+def double(turned):
+    blocks, slab, size = turned.shape
     return pl.pallas_call(
         double_kernel,
-        in_specs=[HBM],
+        in_specs=[VMEM],
         out_specs=HBM,
         out_shape=pltpu.HBM((blocks, 2, slab, size), BF16),
-        scratch_shapes=[
-            pltpu.VMEM(partials.shape, BF16),
-            pltpu.VMEM(partials.shape, BF16),
-            pltpu.SemaphoreType.DMA((4,)),
-            pltpu.SemaphoreType.DMA((8,)),
-        ],
-        compiler_params=params(16),
-    )(far(partials))
+        scratch_shapes=[pltpu.SemaphoreType.DMA((2,))],
+        compiler_params=params(16),
+    )(near(turned))
 
 
 def coded(shampoo, slab, sent, facts, first):
@@ -440,11 +472,12 @@
     side = lax.axis_index("dp")
 
     left = left_root[0]
-    early = lax.ppermute(pack(left, 0), "dp", SWAP)
+    early, turned = front(left, partials)
+    early = lax.ppermute(early, "dp", SWAP)
 
     def deliver(values, left):
         pieces = lax.all_to_all(
-            double(values).reshape(2 * blocks, slab, size),
+            values.reshape(2 * blocks, slab, size),
             ("mp", "dp"),
             split_axis=0,
             concat_axis=0,
@@ -457,7 +490,7 @@
         shapes = jax.eval_shape(lambda: (jnp.zeros((2 * blocks, slab, size), values.dtype), pack(left, 1)))
         return tuple(jnp.zeros(each.shape, each.dtype) for each in shapes)
 
-    pieces, late = lax.cond((side + 2) // 2 == 1, deliver, nothing, partials, left)
+    pieces, late = lax.cond((side + 2) // 2 == 1, deliver, nothing, double(turned), left)
     pieces = pieces.reshape(blocks, 2, slab, size)
     late = lax.ppermute(late, "dp", SWAP)
     where = side.astype(jnp.int32).reshape(1)

time: 118 us -> 117 us (level)
    pallas_call x2 -> x1, Pallas kernels: 4.67 us -> 2.6 us  [pack(): pl.pallas_call(kernel, in_specs=[HBM], out_specs=VMEM, out_shape=jax.Shap...]
    pallas_call x1 -> x2, Pallas kernels: 3.27 us -> 4.28 us  [the longest x1 2.24 us: front(): pl.pallas_call(kernel, in_specs=[HBM, HBM], out_specs=[VMEM, VMEM], out_s...]
  transfers between devices with their start and end apart: 5 -> 5, of which waited for: 4 -> 4; matrix products, arithmetic and copies ran while one was open for 11% -> 11% of each run, Pallas kernels for 14% -> 13%
where the time goes in v2:
time: 117 us; the launch traced here: 116 us
  waiting for transfers between devices  57.3 us (49%)
  starting transfers between devices  23.4 us (20%)
  Pallas kernels  21.8 us (19%)
  matrix products  12.8 us (11%)
    all_to_all x1, waiting for transfers between devices, deliver(): lax.all_to_all(values.reshape(2 * blocks, slab, size), ('mp', 'dp'), spli...  48.2 us
    dot_general x2, matrix products, highest(): jnp.einsum(form, left, right, precision=lax.Precision.HIGH, preferred_ele...  12.8 us
    all_to_all x1, starting transfers between devices, deliver(): lax.all_to_all(values.reshape(2 * blocks, slab, size), ('mp', 'dp'), spli...  11.3 us
    pallas_call x1, Pallas kernels, main(): pl.pallas_call(main_kernel, in_specs=[SMEM, VMEM, HBM, HBM, HBM, VMEM], o...  10.2 us
    all_to_all x1, starting transfers between devices, local(): lax.all_to_all(sent, 'mp', split_axis=0, concat_axis=0, tiled=True, axis_...  9.83 us
    all_to_all x1, waiting for transfers between devices, local(): lax.all_to_all(sent, 'mp', split_axis=0, concat_axis=0, tiled=True, axis_...  5.59 us
    ppermute x1, waiting for transfers between devices, local(): other = lax.ppermute(mine, 'dp', SWAP)  3.14 us
    pallas_call x1, Pallas kernels, pack(): pl.pallas_call(kernel, in_specs=[HBM], out_specs=VMEM, out_shape=jax.Shap...  2.6 us
  transfers between devices with their start and end apart: 5, of which 4 were waited for; matrix products, arithmetic and copies ran while one was open for 11% of the time, Pallas kernels for 13%

profile of v2, /device:TPU:6, one launch (start us, length us, event | category | flops | bytes accessed | tf_op | source)
XLA Modules:
  0.0 116.2 jit_solution(620070304617561797)
XLA Ops:
  0.6 2.2 %shard_map.93 = (bf16[2320,128]{1,0:T(8,128)(2,1)S(1)}, bf16[64,16,1024]{2,1,0:T(8,128)(2,1)S(1)}) custom-call(f32[512,1024]{1,0:T(8,128)} %bitcast.18, bf16[64,16,1024]{2,1,0:T(8,128)(2,1)} %bitcast.21), custom_call_target="tpu_custom_call" | custom-call | tf_op jit(solution)/shard_map/pallas_call | solution.py:128
  2.9 0.9 collective-permute-start
  3.8 2.0 %shard_map.94 = bf16[64,2,16,1024]{3,2,1,0:T(8,128)(2,1)} custom-call(bf16[64,16,1024]{2,1,0:T(8,128)(2,1)S(1)} %get-tuple-element.25.turned_ref), custom_call_target="tpu_custom_call" | custom-call | tf_op jit(solution)/shard_map/pallas_call | solution.py:191
  5.8 0.0 copy-start
  5.8 62.2 %conditional.1 = (bf16[1808,128]{1,0:T(8,128)(2,1)}, bf16[64,2,16,1024]{3,2,1,0:T(8,128)(2,1)}) conditional(s32[]{:T(128)} %convert_element_type.3, () %tuple.19, (f32[512,1024]{1,0:T(8,128)}, bf16[64,2,16,1024]{3,2,1,0:T(8,128)(2,1)}) %tuple.25), branch_computations={%region_0.1_spmd, %region_1.2_spmd} | conditional | bytes 12582960 | solution.py:493
  5.9 11.3 %all-to-all-start = ((bf16[128,16,1024]{2,1,0:T(8,128)(2,1)}), bf16[128,16,1024]{2,1,0:T(8,128)(2,1)}, u32[]{:S(2)}, u32[]{:S(2)}) async-start(bf16[128,16,1024]{2,1,0:T(8,128)(2,1)} %bitcast.17), calls=%async_computation | async-start | bytes 8388608 | tf_op jit(solution)/shard_map/cond/branch_1_fun/all_to_all | solution.py:479
  17.2 2.6 %branch_1_fun.1 = bf16[1808,128]{1,0:T(8,128)(2,1)} custom-call(f32[512,1024]{1,0:T(8,128)} %get-tuple-element.5.refs_0_), custom_call_target="tpu_custom_call" | custom-call | tf_op jit(solution)/shard_map/cond/branch_1_fun/pallas_call | solution.py:154
  19.8 48.2 %all-to-all-done = bf16[128,16,1024]{2,1,0:T(8,128)(2,1)} async-done(((bf16[128,16,1024]{2,1,0:T(8,128)(2,1)}), bf16[128,16,1024]{2,1,0:T(8,128)(2,1)}, u32[]{:S(2)}, u32[]{:S(2)}) %all-to-all-start) | async-done | bytes 4194336 | tf_op jit(solution)/shard_map/cond/branch_1_fun/all_to_all | solution.py:479
  68.0 1.3 %collective-permute-start.1 = (bf16[1808,128]{1,0:T(8,128)(2,1)}, bf16[1808,128]{1,0:T(8,128)(2,1)S(1)}, u32[]{:S(2)}, u32[]{:S(2)}) collective-permute-start(bf16[1808,128]{1,0:T(8,128)(2,1)} %get-tuple-element.30), channel_id=1, source_target_pairs={{0,64},{64,0},{1,65},{65,1},{2,66},{66,2},{3,67},{67,3},{4,68},{68... | collective-permute-start | bytes 1388552 | tf_op jit(solution)/shard_map/ppermute | solution.py:495
  69.3 0.0 collective-permute-done.code_ref
  69.3 0.0 copy-done
  69.3 10.2 %shard_map.95 = (f32[1024,1024]{1,0:T(8,128)}, f32[1024,512]{1,0:T(8,128)}, bf16[64,64,128]{2,1,0:T(8,128)(2,1)S(1)}, bf16[1024,512]{1,0:T(8,128)(2,1)S(1)}, bf1...) custom-call(s32[1]{0:T(128)} %bitcast.2.side_ref, f32[1024,512]{1,0:T(8,128)S(1)} %bitcast.16, ...), custom_call_target="tpu_custom_call" | custom-call | flops 6442450944 | bytes 16777216 | tf_op jit(solution)/shard_map/pallas_call | solution.py:297
  79.6 0.3 collective-permute-done.1.code_ref
  79.9 2.2 %shard_map.96 = bf16[64,80,128]{2,1,0:T(8,128)(2,1)} custom-call(s32[1]{0:T(128)} %bitcast.2.side_ref, bf16[1024,512]{1,0:T(8,128)(2,1)S(1)} %get-tuple-element.28.turn_hi, bf16[1024,512]{1,0:T(8,128)(2,1)S(1)} %get-tuple-element.29.turn_lo, bf16[1808,128]{1,0:T(8,128)(2,1)S(1)} %collective-permute-done.1.code_ref, ...), custom_call_target="tpu_custom_call" | custom-call | flops 704643072 | bytes 4194304 | tf_op jit(solution)/shard_map/pallas_call | solution.py:374
  82.1 0.0 copy-start.2
  82.1 9.8 %all-to-all-start.1 = ((bf16[64,80,128]{2,1,0:T(8,128)(2,1)}), bf16[64,80,128]{2,1,0:T(8,128)(2,1)S(1)}, u32[]{:S(2)}, u32[]{:S(2)}) async-start(bf16[64,80,128]{2,1,0:T(8,128)(2,1)} %shard_map.96), calls=%async_computation.1 | async-start | bytes 2621440 | tf_op jit(solution)/shard_map/all_to_all | solution.py:501
  91.9 0.0 copy-done.2
  92.0 0.0 copy-start.1
  92.0 0.0 copy-start.3
  92.0 7.9 %bitcast_add_fusion = f32[1024,512]{1,0:T(8,128)} fusion(f32[1,1024,512]{2,1,0:T(8,128)S(1)} %copy-done.2, f32[1024,1024]{1,0:T(8,128)} %get-tuple-element.34, s32[]{:T(128)S(6)} %select_n.10), kind=kOutput, calls=%fused_computation | convolution fusion | flops 3222798336 | bytes 10485764 | tf_op jit(solution)/shard_map/ri,rj->ij/dot_general | solution.py:465
  99.9 0.0 copy-done.1
  99.9 0.0 copy-done.3
  99.9 4.9 %bitcast_add_fusion.1 = f32[512,1024]{1,0:T(8,128)} fusion(f32[1,512,1024]{2,1,0:T(8,128)S(1)} %copy-done.3, f32[1024,1024]{1,0:T(8,128)S(1)} %copy-done.1, s32[]{:T(128)S(6)} %select_n.10), kind=kOutput, calls=%fused_computation.1 | convolution fusion | flops 3222798336 | bytes 10485764 | tf_op jit(solution)/shard_map/ic,jc->ij/dot_general | solution.py:465
  104.8 5.6 %all-to-all-done.1.got_ref = bf16[64,80,128]{2,1,0:T(8,128)(2,1)S(1)} async-done(((bf16[64,80,128]{2,1,0:T(8,128)(2,1)}), bf16[64,80,128]{2,1,0:T(8,128)(2,1)S(1)}, u32[]{:S(2)}, u32[]{:S(2)}) %all-to-all-start.1) | async-done | bytes 1310752 | tf_op jit(solution)/shard_map/all_to_all | solution.py:501
  110.4 0.1 collective-permute-start.2
  110.5 0.8 shard_map.97.refs_0_
  111.3 3.1 %collective-permute-done.2.refs_2_ = f32[64,128]{1,0:T(8,128)S(1)} collective-permute-done((f32[64,128]{1,0:T(8,128)S(1)}, f32[64,128]{1,0:T(8,128)S(1)}, u32[]{:S(2)}, u32[]{:S(2)}) %collective-permute-start.2) | collective-permute-done | bytes 32800 | tf_op jit(solution)/shard_map/ppermute | solution.py:511
  114.4 1.7 %shard_map.99 = f32[64,16,512]{2,1,0:T(8,128)} custom-call(f32[64,16,512]{2,1,0:T(8,128)S(1)} %shard_map.97.refs_0_, f32[64,128]{1,0:T(8,128)S(1)} %shard_map.98.refs_1_, f32[64,128]{1,0:T(8,128)S(1)} %collective-permute-done.2.refs_2_), custom_call_target="tpu_custom_call" | custom-call | tf_op jit(solution)/shard_map/pallas_call | solution.py:454
  (1 shorter events, 0.0 us)
Async XLA Ops:
  2.9 66.4 %collective-permute-start = (bf16[2320,128]{1,0:T(8,128)(2,1)S(1)}, bf16[2320,128]{1,0:T(8,128)(2,1)S(1)}, u32[]{:S(2)}, u32[]{:S(2)}) collective-permute-start(bf16[2320,128]{1,0:T(8,128)(2,1)S(1)} %get-tuple-element.27), channel_id=1, source_target_pairs={{0,64},{64,0},{1,65},{65,1},{2,66},{66,2},{3,67},{67,3},{4,68},{68... | collective-permute-start | bytes 1781768 | tf_op jit(solution)/shard_map/ppermute | solution.py:476
  5.8 63.5 %copy-start = (f32[1,1024,512]{2,1,0:T(8,128)S(1)}, f32[1,1024,512]{2,1,0:T(8,128)}, u32[]{:S(2)}) copy-start(f32[1,1024,512]{2,1,0:T(8,128)} %param.11) | copy-start | bytes 6291460
  5.9 62.2 %all-to-all-start = ((bf16[128,16,1024]{2,1,0:T(8,128)(2,1)}), bf16[128,16,1024]{2,1,0:T(8,128)(2,1)}, u32[]{:S(2)}, u32[]{:S(2)}) async-start(bf16[128,16,1024]{2,1,0:T(8,128)(2,1)} %bitcast.17), calls=%async_computation | async-start | bytes 8388608 | tf_op jit(solution)/shard_map/cond/branch_1_fun/all_to_all | solution.py:479
  68.0 11.8 %collective-permute-start.1 = (bf16[1808,128]{1,0:T(8,128)(2,1)}, bf16[1808,128]{1,0:T(8,128)(2,1)S(1)}, u32[]{:S(2)}, u32[]{:S(2)}) collective-permute-start(bf16[1808,128]{1,0:T(8,128)(2,1)} %get-tuple-element.30), channel_id=1, source_target_pairs={{0,64},{64,0},{1,65},{65,1},{2,66},{66,2},{3,67},{67,3},{4,68},{68... | collective-permute-start | bytes 1388552 | tf_op jit(solution)/shard_map/ppermute | solution.py:495
  82.1 9.9 %copy-start.2 = (f32[1,1024,512]{2,1,0:T(8,128)S(1)}, f32[1,1024,512]{2,1,0:T(8,128)}, u32[]{:S(2)}) copy-start(f32[1,1024,512]{2,1,0:T(8,128)} %param.13) | copy-start | bytes 6291460
  82.1 28.3 %all-to-all-start.1 = ((bf16[64,80,128]{2,1,0:T(8,128)(2,1)}), bf16[64,80,128]{2,1,0:T(8,128)(2,1)S(1)}, u32[]{:S(2)}, u32[]{:S(2)}) async-start(bf16[64,80,128]{2,1,0:T(8,128)(2,1)} %shard_map.96), calls=%async_computation.1 | async-start | bytes 2621440 | tf_op jit(solution)/shard_map/all_to_all | solution.py:501
  92.0 7.9 %copy-start.1 = (f32[1024,1024]{1,0:T(8,128)S(1)}, f32[1024,1024]{1,0:T(8,128)}, u32[]{:S(2)}) copy-start(f32[1024,1024]{1,0:T(8,128)} %get-tuple-element.34) | copy-start | bytes 12582916
  92.0 7.9 %copy-start.3 = (f32[1,512,1024]{2,1,0:T(8,128)S(1)}, f32[1,512,1024]{2,1,0:T(8,128)}, u32[]{:S(2)}) copy-start(f32[1,512,1024]{2,1,0:T(8,128)} %param.12) | copy-start | bytes 6291460
  110.4 4.0 %collective-permute-start.2 = (f32[64,128]{1,0:T(8,128)S(1)}, f32[64,128]{1,0:T(8,128)S(1)}, u32[]{:S(2)}, u32[]{:S(2)}) collective-permute-start(f32[64,128]{1,0:T(8,128)S(1)} %shard_map.98.refs_1_), channel_id=1, source_target_pairs={{0,64},{64,0},{1,65},{65,1},{2,66},{66,2},{3,67},{67,3},{4,68},{68... | collective-permute-start | bytes 98312 | tf_op jit(solution)/shard_map/ppermute | solution.py:511

commit v3 on v2

--- a/solution.py
+++ b/solution.py
@@ -269,7 +269,7 @@
         moment_arrivals[chunk].wait()
         moment_new = MOMENT_DECAY * moment[here] + (1.0 - MOMENT_DECAY) * mine * mine
         new[here] = moment_new
-        direction = mine / (jnp.sqrt(moment_new) + ADAM_EPS)
+        direction = mine / (moment_new * lax.rsqrt(moment_new) + ADAM_EPS)
         adam += fold(direction * direction)
     write(new, new_ref)
 

time: 117 us -> 116 us (level)
  no operation moved by 1% of the time
where the time goes in v3:
time: 116 us
  waiting for transfers between devices  57.5 us (50%)
  starting transfers between devices  23.1 us (20%)
  Pallas kernels  21.5 us (19%)
  matrix products  12.8 us (11%)
    all_to_all x1, waiting for transfers between devices, deliver(): lax.all_to_all(values.reshape(2 * blocks, slab, size), ('mp', 'dp'), spli...  48.2 us
    dot_general x2, matrix products, highest(): jnp.einsum(form, left, right, precision=lax.Precision.HIGH, preferred_ele...  12.8 us
    all_to_all x1, starting transfers between devices, deliver(): lax.all_to_all(values.reshape(2 * blocks, slab, size), ('mp', 'dp'), spli...  11.3 us
    pallas_call x1, Pallas kernels, main(): pl.pallas_call(main_kernel, in_specs=[SMEM, VMEM, HBM, HBM, HBM, VMEM], o...  9.91 us
    all_to_all x1, starting transfers between devices, local(): lax.all_to_all(sent, 'mp', split_axis=0, concat_axis=0, tiled=True, axis_...  9.41 us
    all_to_all x1, waiting for transfers between devices, local(): lax.all_to_all(sent, 'mp', split_axis=0, concat_axis=0, tiled=True, axis_...  5.59 us
    ppermute x1, waiting for transfers between devices, local(): other = lax.ppermute(mine, 'dp', SWAP)  3.03 us
    pallas_call x1, Pallas kernels, pack(): pl.pallas_call(kernel, in_specs=[HBM], out_specs=VMEM, out_shape=jax.Shap...  2.6 us
  transfers between devices with their start and end apart: 5, of which 4 were waited for; matrix products, arithmetic and copies ran while one was open for 11% of the time, Pallas kernels for 13%

profile of v3, /device:TPU:6, one launch (start us, length us, event | category | flops | bytes accessed | tf_op | source)
XLA Modules:
  0.0 115.8 jit_solution(8977020329201497361)
XLA Ops:
  0.6 2.2 %shard_map.93 = (bf16[2320,128]{1,0:T(8,128)(2,1)S(1)}, bf16[64,16,1024]{2,1,0:T(8,128)(2,1)S(1)}) custom-call(f32[512,1024]{1,0:T(8,128)} %bitcast.18, bf16[64,16,1024]{2,1,0:T(8,128)(2,1)} %bitcast.21), custom_call_target="tpu_custom_call" | custom-call | tf_op jit(solution)/shard_map/pallas_call | solution.py:128
  2.9 0.9 collective-permute-start
  3.8 2.0 %shard_map.94 = bf16[64,2,16,1024]{3,2,1,0:T(8,128)(2,1)} custom-call(bf16[64,16,1024]{2,1,0:T(8,128)(2,1)S(1)} %get-tuple-element.25.turned_ref), custom_call_target="tpu_custom_call" | custom-call | tf_op jit(solution)/shard_map/pallas_call | solution.py:191
  5.8 0.0 copy-start
  5.8 62.2 %conditional.1 = (bf16[1808,128]{1,0:T(8,128)(2,1)}, bf16[64,2,16,1024]{3,2,1,0:T(8,128)(2,1)}) conditional(s32[]{:T(128)} %convert_element_type.3, () %tuple.19, (f32[512,1024]{1,0:T(8,128)}, bf16[64,2,16,1024]{3,2,1,0:T(8,128)(2,1)}) %tuple.25), branch_computations={%region_0.1_spmd, %region_1.2_spmd} | conditional | bytes 12582960 | solution.py:493
  5.9 11.3 %all-to-all-start = ((bf16[128,16,1024]{2,1,0:T(8,128)(2,1)}), bf16[128,16,1024]{2,1,0:T(8,128)(2,1)}, u32[]{:S(2)}, u32[]{:S(2)}) async-start(bf16[128,16,1024]{2,1,0:T(8,128)(2,1)} %bitcast.17), calls=%async_computation | async-start | bytes 8388608 | tf_op jit(solution)/shard_map/cond/branch_1_fun/all_to_all | solution.py:479
  17.2 2.6 %branch_1_fun.1 = bf16[1808,128]{1,0:T(8,128)(2,1)} custom-call(f32[512,1024]{1,0:T(8,128)} %get-tuple-element.5.refs_0_), custom_call_target="tpu_custom_call" | custom-call | tf_op jit(solution)/shard_map/cond/branch_1_fun/pallas_call | solution.py:154
  19.8 48.2 %all-to-all-done = bf16[128,16,1024]{2,1,0:T(8,128)(2,1)} async-done(((bf16[128,16,1024]{2,1,0:T(8,128)(2,1)}), bf16[128,16,1024]{2,1,0:T(8,128)(2,1)}, u32[]{:S(2)}, u32[]{:S(2)}) %all-to-all-start) | async-done | bytes 4194336 | tf_op jit(solution)/shard_map/cond/branch_1_fun/all_to_all | solution.py:479
  68.0 1.3 %collective-permute-start.1 = (bf16[1808,128]{1,0:T(8,128)(2,1)}, bf16[1808,128]{1,0:T(8,128)(2,1)S(1)}, u32[]{:S(2)}, u32[]{:S(2)}) collective-permute-start(bf16[1808,128]{1,0:T(8,128)(2,1)} %get-tuple-element.30), channel_id=1, source_target_pairs={{0,64},{64,0},{1,65},{65,1},{2,66},{66,2},{3,67},{67,3},{4,68},{68... | collective-permute-start | bytes 1388552 | tf_op jit(solution)/shard_map/ppermute | solution.py:495
  69.3 0.0 collective-permute-done.code_ref
  69.3 0.0 copy-done
  69.3 9.9 %shard_map.95 = (f32[1024,1024]{1,0:T(8,128)}, f32[1024,512]{1,0:T(8,128)}, bf16[64,64,128]{2,1,0:T(8,128)(2,1)S(1)}, bf16[1024,512]{1,0:T(8,128)(2,1)S(1)}, bf1...) custom-call(s32[1]{0:T(128)} %bitcast.2.side_ref, f32[1024,512]{1,0:T(8,128)S(1)} %bitcast.16, ...), custom_call_target="tpu_custom_call" | custom-call | flops 6442450944 | bytes 16777216 | tf_op jit(solution)/shard_map/pallas_call | solution.py:297
  79.2 0.6 collective-permute-done.1.code_ref
  79.9 2.2 %shard_map.96 = bf16[64,80,128]{2,1,0:T(8,128)(2,1)} custom-call(s32[1]{0:T(128)} %bitcast.2.side_ref, bf16[1024,512]{1,0:T(8,128)(2,1)S(1)} %get-tuple-element.28.turn_hi, bf16[1024,512]{1,0:T(8,128)(2,1)S(1)} %get-tuple-element.29.turn_lo, bf16[1808,128]{1,0:T(8,128)(2,1)S(1)} %collective-permute-done.1.code_ref, ...), custom_call_target="tpu_custom_call" | custom-call | flops 704643072 | bytes 4194304 | tf_op jit(solution)/shard_map/pallas_call | solution.py:374
  82.1 0.0 copy-start.2
  82.1 9.4 %all-to-all-start.1 = ((bf16[64,80,128]{2,1,0:T(8,128)(2,1)}), bf16[64,80,128]{2,1,0:T(8,128)(2,1)S(1)}, u32[]{:S(2)}, u32[]{:S(2)}) async-start(bf16[64,80,128]{2,1,0:T(8,128)(2,1)} %shard_map.96), calls=%async_computation.1 | async-start | bytes 2621440 | tf_op jit(solution)/shard_map/all_to_all | solution.py:501
  91.5 0.0 copy-done.2
  91.5 0.0 copy-start.1
  91.5 0.0 copy-start.3
  91.6 7.9 %bitcast_add_fusion = f32[1024,512]{1,0:T(8,128)} fusion(f32[1,1024,512]{2,1,0:T(8,128)S(1)} %copy-done.2, f32[1024,1024]{1,0:T(8,128)} %get-tuple-element.34, s32[]{:T(128)S(6)} %select_n.10), kind=kOutput, calls=%fused_computation | convolution fusion | flops 3222798336 | bytes 10485764 | tf_op jit(solution)/shard_map/ri,rj->ij/dot_general | solution.py:465
  99.4 0.0 copy-done.1
  99.4 0.0 copy-done.3
  99.4 4.9 %bitcast_add_fusion.1 = f32[512,1024]{1,0:T(8,128)} fusion(f32[1,512,1024]{2,1,0:T(8,128)S(1)} %copy-done.3, f32[1024,1024]{1,0:T(8,128)S(1)} %copy-done.1, s32[]{:T(128)S(6)} %select_n.10), kind=kOutput, calls=%fused_computation.1 | convolution fusion | flops 3222798336 | bytes 10485764 | tf_op jit(solution)/shard_map/ic,jc->ij/dot_general | solution.py:465
  104.4 5.6 %all-to-all-done.1.got_ref = bf16[64,80,128]{2,1,0:T(8,128)(2,1)S(1)} async-done(((bf16[64,80,128]{2,1,0:T(8,128)(2,1)}), bf16[64,80,128]{2,1,0:T(8,128)(2,1)S(1)}, u32[]{:S(2)}, u32[]{:S(2)}) %all-to-all-start.1) | async-done | bytes 1310752 | tf_op jit(solution)/shard_map/all_to_all | solution.py:501
  110.0 0.2 collective-permute-start.2
  110.2 0.8 shard_map.97.refs_0_
  110.9 3.0 %collective-permute-done.2.refs_2_ = f32[64,128]{1,0:T(8,128)S(1)} collective-permute-done((f32[64,128]{1,0:T(8,128)S(1)}, f32[64,128]{1,0:T(8,128)S(1)}, u32[]{:S(2)}, u32[]{:S(2)}) %collective-permute-start.2) | collective-permute-done | bytes 32800 | tf_op jit(solution)/shard_map/ppermute | solution.py:511
  114.0 1.7 %shard_map.99 = f32[64,16,512]{2,1,0:T(8,128)} custom-call(f32[64,16,512]{2,1,0:T(8,128)S(1)} %shard_map.97.refs_0_, f32[64,128]{1,0:T(8,128)S(1)} %shard_map.98.refs_1_, f32[64,128]{1,0:T(8,128)S(1)} %collective-permute-done.2.refs_2_), custom_call_target="tpu_custom_call" | custom-call | tf_op jit(solution)/shard_map/pallas_call | solution.py:454
  (1 shorter events, 0.0 us)
Async XLA Ops:
  2.9 66.4 %collective-permute-start = (bf16[2320,128]{1,0:T(8,128)(2,1)S(1)}, bf16[2320,128]{1,0:T(8,128)(2,1)S(1)}, u32[]{:S(2)}, u32[]{:S(2)}) collective-permute-start(bf16[2320,128]{1,0:T(8,128)(2,1)S(1)} %get-tuple-element.27), channel_id=1, source_target_pairs={{0,64},{64,0},{1,65},{65,1},{2,66},{66,2},{3,67},{67,3},{4,68},{68... | collective-permute-start | bytes 1781768 | tf_op jit(solution)/shard_map/ppermute | solution.py:476
  5.8 63.5 %copy-start = (f32[1,1024,512]{2,1,0:T(8,128)S(1)}, f32[1,1024,512]{2,1,0:T(8,128)}, u32[]{:S(2)}) copy-start(f32[1,1024,512]{2,1,0:T(8,128)} %param.11) | copy-start | bytes 6291460
  5.9 62.2 %all-to-all-start = ((bf16[128,16,1024]{2,1,0:T(8,128)(2,1)}), bf16[128,16,1024]{2,1,0:T(8,128)(2,1)}, u32[]{:S(2)}, u32[]{:S(2)}) async-start(bf16[128,16,1024]{2,1,0:T(8,128)(2,1)} %bitcast.17), calls=%async_computation | async-start | bytes 8388608 | tf_op jit(solution)/shard_map/cond/branch_1_fun/all_to_all | solution.py:479
  68.0 11.8 %collective-permute-start.1 = (bf16[1808,128]{1,0:T(8,128)(2,1)}, bf16[1808,128]{1,0:T(8,128)(2,1)S(1)}, u32[]{:S(2)}, u32[]{:S(2)}) collective-permute-start(bf16[1808,128]{1,0:T(8,128)(2,1)} %get-tuple-element.30), channel_id=1, source_target_pairs={{0,64},{64,0},{1,65},{65,1},{2,66},{66,2},{3,67},{67,3},{4,68},{68... | collective-permute-start | bytes 1388552 | tf_op jit(solution)/shard_map/ppermute | solution.py:495
  82.1 9.4 %copy-start.2 = (f32[1,1024,512]{2,1,0:T(8,128)S(1)}, f32[1,1024,512]{2,1,0:T(8,128)}, u32[]{:S(2)}) copy-start(f32[1,1024,512]{2,1,0:T(8,128)} %param.13) | copy-start | bytes 6291460
  82.1 27.8 %all-to-all-start.1 = ((bf16[64,80,128]{2,1,0:T(8,128)(2,1)}), bf16[64,80,128]{2,1,0:T(8,128)(2,1)S(1)}, u32[]{:S(2)}, u32[]{:S(2)}) async-start(bf16[64,80,128]{2,1,0:T(8,128)(2,1)} %shard_map.96), calls=%async_computation.1 | async-start | bytes 2621440 | tf_op jit(solution)/shard_map/all_to_all | solution.py:501
  91.5 7.9 %copy-start.1 = (f32[1024,1024]{1,0:T(8,128)S(1)}, f32[1024,1024]{1,0:T(8,128)}, u32[]{:S(2)}) copy-start(f32[1024,1024]{1,0:T(8,128)} %get-tuple-element.34) | copy-start | bytes 12582916
  91.5 7.9 %copy-start.3 = (f32[1,512,1024]{2,1,0:T(8,128)S(1)}, f32[1,512,1024]{2,1,0:T(8,128)}, u32[]{:S(2)}) copy-start(f32[1,512,1024]{2,1,0:T(8,128)} %param.12) | copy-start | bytes 6291460
  110.0 4.0 %collective-permute-start.2 = (f32[64,128]{1,0:T(8,128)S(1)}, f32[64,128]{1,0:T(8,128)S(1)}, u32[]{:S(2)}, u32[]{:S(2)}) collective-permute-start(f32[64,128]{1,0:T(8,128)S(1)} %shard_map.98.refs_1_), channel_id=1, source_target_pairs={{0,64},{64,0},{1,65},{65,1},{2,66},{66,2},{3,67},{67,3},{4,68},{68... | collective-permute-start | bytes 98312 | tf_op jit(solution)/shard_map/ppermute | solution.py:511

commit v4 on v3

--- a/solution.py
+++ b/solution.py
@@ -456,7 +456,7 @@
         in_specs=[VMEM] * 3,
         out_specs=ANY,
         out_shape=jax.ShapeDtypeStruct(values.shape, F32),
-        scratch_shapes=[pltpu.VMEM(values.shape, F32), pltpu.SemaphoreType.DMA((4,))],
+        scratch_shapes=[pltpu.VMEM(values.shape, F32), pltpu.SemaphoreType.DMA((8,))],
         compiler_params=params(16),
     )(near(values), mine, other)
 

time: 116 us -> 116 us (level)
  no operation moved by 1% of the time
where the time goes in v4:
time: 116 us
  waiting for transfers between devices  57.5 us (50%)
  starting transfers between devices  23.1 us (20%)
  Pallas kernels  21.5 us (19%)
  matrix products  12.8 us (11%)
    all_to_all x1, waiting for transfers between devices, deliver(): lax.all_to_all(values.reshape(2 * blocks, slab, size), ('mp', 'dp'), spli...  48.2 us
    dot_general x2, matrix products, highest(): jnp.einsum(form, left, right, precision=lax.Precision.HIGH, preferred_ele...  12.8 us
    all_to_all x1, starting transfers between devices, deliver(): lax.all_to_all(values.reshape(2 * blocks, slab, size), ('mp', 'dp'), spli...  11.3 us
    pallas_call x1, Pallas kernels, main(): pl.pallas_call(main_kernel, in_specs=[SMEM, VMEM, HBM, HBM, HBM, VMEM], o...  9.91 us
    all_to_all x1, starting transfers between devices, local(): lax.all_to_all(sent, 'mp', split_axis=0, concat_axis=0, tiled=True, axis_...  9.41 us
    all_to_all x1, waiting for transfers between devices, local(): lax.all_to_all(sent, 'mp', split_axis=0, concat_axis=0, tiled=True, axis_...  5.59 us
    ppermute x1, waiting for transfers between devices, local(): other = lax.ppermute(mine, 'dp', SWAP)  3.03 us
    pallas_call x1, Pallas kernels, pack(): pl.pallas_call(kernel, in_specs=[HBM], out_specs=VMEM, out_shape=jax.Shap...  2.6 us
  transfers between devices with their start and end apart: 5, of which 4 were waited for; matrix products, arithmetic and copies ran while one was open for 11% of the time, Pallas kernels for 13%

profile of v4, /device:TPU:6, one launch (start us, length us, event | category | flops | bytes accessed | tf_op | source)
XLA Modules:
  0.0 115.8 jit_solution(10753050560715701897)
XLA Ops:
  0.6 2.2 %shard_map.93 = (bf16[2320,128]{1,0:T(8,128)(2,1)S(1)}, bf16[64,16,1024]{2,1,0:T(8,128)(2,1)S(1)}) custom-call(f32[512,1024]{1,0:T(8,128)} %bitcast.18, bf16[64,16,1024]{2,1,0:T(8,128)(2,1)} %bitcast.21), custom_call_target="tpu_custom_call" | custom-call | tf_op jit(solution)/shard_map/pallas_call | solution.py:128
  2.9 0.9 collective-permute-start
  3.8 2.0 %shard_map.94 = bf16[64,2,16,1024]{3,2,1,0:T(8,128)(2,1)} custom-call(bf16[64,16,1024]{2,1,0:T(8,128)(2,1)S(1)} %get-tuple-element.25.turned_ref), custom_call_target="tpu_custom_call" | custom-call | tf_op jit(solution)/shard_map/pallas_call | solution.py:191
  5.8 0.0 copy-start
  5.8 62.2 %conditional.1 = (bf16[1808,128]{1,0:T(8,128)(2,1)}, bf16[64,2,16,1024]{3,2,1,0:T(8,128)(2,1)}) conditional(s32[]{:T(128)} %convert_element_type.3, () %tuple.19, (f32[512,1024]{1,0:T(8,128)}, bf16[64,2,16,1024]{3,2,1,0:T(8,128)(2,1)}) %tuple.25), branch_computations={%region_0.1_spmd, %region_1.2_spmd} | conditional | bytes 12582960 | solution.py:493
  5.9 11.3 %all-to-all-start = ((bf16[128,16,1024]{2,1,0:T(8,128)(2,1)}), bf16[128,16,1024]{2,1,0:T(8,128)(2,1)}, u32[]{:S(2)}, u32[]{:S(2)}) async-start(bf16[128,16,1024]{2,1,0:T(8,128)(2,1)} %bitcast.17), calls=%async_computation | async-start | bytes 8388608 | tf_op jit(solution)/shard_map/cond/branch_1_fun/all_to_all | solution.py:479
  17.2 2.6 %branch_1_fun.1 = bf16[1808,128]{1,0:T(8,128)(2,1)} custom-call(f32[512,1024]{1,0:T(8,128)} %get-tuple-element.5.refs_0_), custom_call_target="tpu_custom_call" | custom-call | tf_op jit(solution)/shard_map/cond/branch_1_fun/pallas_call | solution.py:154
  19.8 48.2 %all-to-all-done = bf16[128,16,1024]{2,1,0:T(8,128)(2,1)} async-done(((bf16[128,16,1024]{2,1,0:T(8,128)(2,1)}), bf16[128,16,1024]{2,1,0:T(8,128)(2,1)}, u32[]{:S(2)}, u32[]{:S(2)}) %all-to-all-start) | async-done | bytes 4194336 | tf_op jit(solution)/shard_map/cond/branch_1_fun/all_to_all | solution.py:479
  68.0 1.3 %collective-permute-start.1 = (bf16[1808,128]{1,0:T(8,128)(2,1)}, bf16[1808,128]{1,0:T(8,128)(2,1)S(1)}, u32[]{:S(2)}, u32[]{:S(2)}) collective-permute-start(bf16[1808,128]{1,0:T(8,128)(2,1)} %get-tuple-element.30), channel_id=1, source_target_pairs={{0,64},{64,0},{1,65},{65,1},{2,66},{66,2},{3,67},{67,3},{4,68},{68... | collective-permute-start | bytes 1388552 | tf_op jit(solution)/shard_map/ppermute | solution.py:495
  69.3 0.0 collective-permute-done.code_ref
  69.3 0.0 copy-done
  69.3 9.9 %shard_map.95 = (f32[1024,1024]{1,0:T(8,128)}, f32[1024,512]{1,0:T(8,128)}, bf16[64,64,128]{2,1,0:T(8,128)(2,1)S(1)}, bf16[1024,512]{1,0:T(8,128)(2,1)S(1)}, bf1...) custom-call(s32[1]{0:T(128)} %bitcast.2.side_ref, f32[1024,512]{1,0:T(8,128)S(1)} %bitcast.16, ...), custom_call_target="tpu_custom_call" | custom-call | flops 6442450944 | bytes 16777216 | tf_op jit(solution)/shard_map/pallas_call | solution.py:297
  79.2 0.6 collective-permute-done.1.code_ref
  79.9 2.2 %shard_map.96 = bf16[64,80,128]{2,1,0:T(8,128)(2,1)} custom-call(s32[1]{0:T(128)} %bitcast.2.side_ref, bf16[1024,512]{1,0:T(8,128)(2,1)S(1)} %get-tuple-element.28.turn_hi, bf16[1024,512]{1,0:T(8,128)(2,1)S(1)} %get-tuple-element.29.turn_lo, bf16[1808,128]{1,0:T(8,128)(2,1)S(1)} %collective-permute-done.1.code_ref, ...), custom_call_target="tpu_custom_call" | custom-call | flops 704643072 | bytes 4194304 | tf_op jit(solution)/shard_map/pallas_call | solution.py:374
  82.1 0.0 copy-start.2
  82.1 9.4 %all-to-all-start.1 = ((bf16[64,80,128]{2,1,0:T(8,128)(2,1)}), bf16[64,80,128]{2,1,0:T(8,128)(2,1)S(1)}, u32[]{:S(2)}, u32[]{:S(2)}) async-start(bf16[64,80,128]{2,1,0:T(8,128)(2,1)} %shard_map.96), calls=%async_computation.1 | async-start | bytes 2621440 | tf_op jit(solution)/shard_map/all_to_all | solution.py:501
  91.5 0.0 copy-done.2
  91.5 0.0 copy-start.1
  91.5 0.0 copy-start.3
  91.6 7.9 %bitcast_add_fusion = f32[1024,512]{1,0:T(8,128)} fusion(f32[1,1024,512]{2,1,0:T(8,128)S(1)} %copy-done.2, f32[1024,1024]{1,0:T(8,128)} %get-tuple-element.34, s32[]{:T(128)S(6)} %select_n.10), kind=kOutput, calls=%fused_computation | convolution fusion | flops 3222798336 | bytes 10485764 | tf_op jit(solution)/shard_map/ri,rj->ij/dot_general | solution.py:465
  99.4 0.0 copy-done.1
  99.4 0.0 copy-done.3
  99.4 4.9 %bitcast_add_fusion.1 = f32[512,1024]{1,0:T(8,128)} fusion(f32[1,512,1024]{2,1,0:T(8,128)S(1)} %copy-done.3, f32[1024,1024]{1,0:T(8,128)S(1)} %copy-done.1, s32[]{:T(128)S(6)} %select_n.10), kind=kOutput, calls=%fused_computation.1 | convolution fusion | flops 3222798336 | bytes 10485764 | tf_op jit(solution)/shard_map/ic,jc->ij/dot_general | solution.py:465
  104.4 5.6 %all-to-all-done.1.got_ref = bf16[64,80,128]{2,1,0:T(8,128)(2,1)S(1)} async-done(((bf16[64,80,128]{2,1,0:T(8,128)(2,1)}), bf16[64,80,128]{2,1,0:T(8,128)(2,1)S(1)}, u32[]{:S(2)}, u32[]{:S(2)}) %all-to-all-start.1) | async-done | bytes 1310752 | tf_op jit(solution)/shard_map/all_to_all | solution.py:501
  110.0 0.2 collective-permute-start.2
  110.2 0.8 shard_map.97.refs_0_
  110.9 3.0 %collective-permute-done.2.refs_2_ = f32[64,128]{1,0:T(8,128)S(1)} collective-permute-done((f32[64,128]{1,0:T(8,128)S(1)}, f32[64,128]{1,0:T(8,128)S(1)}, u32[]{:S(2)}, u32[]{:S(2)}) %collective-permute-start.2) | collective-permute-done | bytes 32800 | tf_op jit(solution)/shard_map/ppermute | solution.py:511
  114.0 1.7 %shard_map.99 = f32[64,16,512]{2,1,0:T(8,128)} custom-call(f32[64,16,512]{2,1,0:T(8,128)S(1)} %shard_map.97.refs_0_, f32[64,128]{1,0:T(8,128)S(1)} %shard_map.98.refs_1_, f32[64,128]{1,0:T(8,128)S(1)} %collective-permute-done.2.refs_2_), custom_call_target="tpu_custom_call" | custom-call | tf_op jit(solution)/shard_map/pallas_call | solution.py:454
  (1 shorter events, 0.0 us)
Async XLA Ops:
  2.9 66.4 %collective-permute-start = (bf16[2320,128]{1,0:T(8,128)(2,1)S(1)}, bf16[2320,128]{1,0:T(8,128)(2,1)S(1)}, u32[]{:S(2)}, u32[]{:S(2)}) collective-permute-start(bf16[2320,128]{1,0:T(8,128)(2,1)S(1)} %get-tuple-element.27), channel_id=1, source_target_pairs={{0,64},{64,0},{1,65},{65,1},{2,66},{66,2},{3,67},{67,3},{4,68},{68... | collective-permute-start | bytes 1781768 | tf_op jit(solution)/shard_map/ppermute | solution.py:476
  5.8 63.5 %copy-start = (f32[1,1024,512]{2,1,0:T(8,128)S(1)}, f32[1,1024,512]{2,1,0:T(8,128)}, u32[]{:S(2)}) copy-start(f32[1,1024,512]{2,1,0:T(8,128)} %param.11) | copy-start | bytes 6291460
  5.9 62.2 %all-to-all-start = ((bf16[128,16,1024]{2,1,0:T(8,128)(2,1)}), bf16[128,16,1024]{2,1,0:T(8,128)(2,1)}, u32[]{:S(2)}, u32[]{:S(2)}) async-start(bf16[128,16,1024]{2,1,0:T(8,128)(2,1)} %bitcast.17), calls=%async_computation | async-start | bytes 8388608 | tf_op jit(solution)/shard_map/cond/branch_1_fun/all_to_all | solution.py:479
  68.0 11.8 %collective-permute-start.1 = (bf16[1808,128]{1,0:T(8,128)(2,1)}, bf16[1808,128]{1,0:T(8,128)(2,1)S(1)}, u32[]{:S(2)}, u32[]{:S(2)}) collective-permute-start(bf16[1808,128]{1,0:T(8,128)(2,1)} %get-tuple-element.30), channel_id=1, source_target_pairs={{0,64},{64,0},{1,65},{65,1},{2,66},{66,2},{3,67},{67,3},{4,68},{68... | collective-permute-start | bytes 1388552 | tf_op jit(solution)/shard_map/ppermute | solution.py:495
  82.1 9.4 %copy-start.2 = (f32[1,1024,512]{2,1,0:T(8,128)S(1)}, f32[1,1024,512]{2,1,0:T(8,128)}, u32[]{:S(2)}) copy-start(f32[1,1024,512]{2,1,0:T(8,128)} %param.13) | copy-start | bytes 6291460
  82.1 27.8 %all-to-all-start.1 = ((bf16[64,80,128]{2,1,0:T(8,128)(2,1)}), bf16[64,80,128]{2,1,0:T(8,128)(2,1)S(1)}, u32[]{:S(2)}, u32[]{:S(2)}) async-start(bf16[64,80,128]{2,1,0:T(8,128)(2,1)} %shard_map.96), calls=%async_computation.1 | async-start | bytes 2621440 | tf_op jit(solution)/shard_map/all_to_all | solution.py:501
  91.5 7.9 %copy-start.1 = (f32[1024,1024]{1,0:T(8,128)S(1)}, f32[1024,1024]{1,0:T(8,128)}, u32[]{:S(2)}) copy-start(f32[1024,1024]{1,0:T(8,128)} %get-tuple-element.34) | copy-start | bytes 12582916
  91.5 7.9 %copy-start.3 = (f32[1,512,1024]{2,1,0:T(8,128)S(1)}, f32[1,512,1024]{2,1,0:T(8,128)}, u32[]{:S(2)}) copy-start(f32[1,512,1024]{2,1,0:T(8,128)} %param.12) | copy-start | bytes 6291460
  110.0 4.0 %collective-permute-start.2 = (f32[64,128]{1,0:T(8,128)S(1)}, f32[64,128]{1,0:T(8,128)S(1)}, u32[]{:S(2)}, u32[]{:S(2)}) collective-permute-start(f32[64,128]{1,0:T(8,128)S(1)} %shard_map.98.refs_1_), channel_id=1, source_target_pairs={{0,64},{64,0},{1,65},{65,1},{2,66},{66,2},{3,67},{67,3},{4,68},{68... | collective-permute-start | bytes 98312 | tf_op jit(solution)/shard_map/ppermute | solution.py:511
